TPU v7x, 256 devices: a whole 4x4x8 slice. The times are simulated.
256 devices in a mesh: dp: 32 (over z, y), mem: 8 (over x, core).
Axes of the slice: x: 4, y: 4, z: 8, core: 2. Of those that a mesh axis runs over, the one named last changes fastest.
Arguments:
- modelled_reactions: bfloat16 [98304, 2048], P('dp', 'mem'), may hold values from -6 to 6
- observations: float32 [98304], P('dp'), may hold values from -6 to 6
- noise_class: int32 [98304], P('dp'), may hold values from 0 to 7
- class_variance: float32 [8], replicated, may hold values from 0.25 to 4
- ensemble: float32 [64, 2048], P(None, 'mem'), may hold values from -18 to 18
Outputs:
- updated: float32 [64, 2048], P(None, 'mem')
All inputs are finite; a program needn't handle non-finite values.
Results may differ from a plain program's by a relative error of at most 0.0003.
The roundings to bfloat16 on the way count: a program that leaves them out, or rounds other values in their place, can miss the bound.
Values may be sent and summed in bfloat16 or wider, within the bound.
A program may use at most 64 MiB of HBM per device.

v0:
```python
import math

import jax
import jax.numpy as jnp
from jax import lax
from jax.sharding import PartitionSpec as P

ITERS = 2


def shards(modelled_reactions, observations, noise_class, class_variance, ensemble):
    row_count, col_count = modelled_reactions.shape
    members = col_count * lax.axis_size("mem")
    band_rows = members // lax.axis_size("dp")
    dp_index = lax.axis_index("dp")
    mem_index = lax.axis_index("mem")
    levels = jnp.arange(class_variance.shape[0], dtype=jnp.int32)
    variance = jnp.sum(
        jnp.where(noise_class[:, None] == levels[None, :], class_variance[None, :], 0.0), axis=1
    )
    weight = lax.rsqrt(variance)
    prior_parameter_vector = modelled_reactions.astype(jnp.float32)
    sample_aggregate = lax.psum(jnp.sum(prior_parameter_vector, axis=1), "mem")
    sample_average = sample_aggregate / members
    normalised_deviation = weight / math.sqrt(members - 1)
    decorrelated_lines = (
        (prior_parameter_vector - sample_average[:, None]) * normalised_deviation[:, None]
    ).astype(jnp.bfloat16)
    innovation = weight * (observations - sample_average)
    projected = lax.psum(
        jnp.dot(
            innovation, decorrelated_lines.astype(jnp.float32), precision=lax.Precision.HIGHEST
        ),
        "dp",
    )
    gathered = lax.all_gather(ensemble, "mem", axis=1, tiled=True)
    row_ids = dp_index * band_rows + jnp.arange(band_rows, dtype=jnp.int32)
    col_ids = mem_index * col_count + jnp.arange(col_count, dtype=jnp.int32)
    identity = (row_ids[:, None] == col_ids[None, :]).astype(jnp.float32)
    strip = lax.dot_general(
        lax.all_gather(decorrelated_lines, "mem", axis=1, tiled=True),
        decorrelated_lines,
        (((0,), (0,)), ((), ())),
        preferred_element_type=jnp.float32,
    )
    gram = lax.psum_scatter(strip, "dp", scatter_dimension=0, tiled=True)
    total = lax.psum(jnp.sum(gram * identity), ("dp", "mem"))
    norm_scale = (members + total) / members
    current = (gram + identity) / norm_scale
    inverse = identity
    for sweep in range(ITERS):
        current_rows, inverse_rows = (
            lax.all_gather(current, "mem", axis=1, tiled=True),
            lax.all_gather(inverse, "mem", axis=1, tiled=True),
        )
        product = jnp.dot(
            inverse_rows,
            lax.all_gather(current, "dp", axis=0, tiled=True),
            precision=lax.Precision.HIGHEST,
        )
        update = 1.5 * identity - 0.5 * product
        piece = lax.all_gather(update, "dp", axis=0, tiled=True)
        current = jnp.dot(current_rows, piece, precision=lax.Precision.HIGHEST)
        inverse = jnp.dot(inverse_rows, piece, precision=lax.Precision.HIGHEST)
    center = jnp.sum(gathered, axis=1) / members
    anomaly = gathered - center[:, None]
    band_anomaly = lax.dynamic_slice_in_dim(anomaly, dp_index * band_rows, band_rows, 1)
    own_anomaly = lax.dynamic_slice_in_dim(anomaly, mem_index * col_count, col_count, 1)
    weighted = lax.psum(jnp.dot(inverse, projected, precision=lax.Precision.HIGHEST), "mem")
    moved_part = jnp.dot(band_anomaly, inverse, precision=lax.Precision.HIGHEST)
    share_part = jnp.dot(weighted, inverse, precision=lax.Precision.HIGHEST)
    moved, shares = lax.psum((moved_part, share_part), "dp")
    shares = shares / norm_scale
    shift = lax.psum(
        jnp.dot(own_anomaly, shares, precision=lax.Precision.HIGHEST), "mem"
    ) / math.sqrt(members - 1)
    return center[:, None] + shift[:, None] + moved / jnp.sqrt(norm_scale)


def solution(mesh):
    placed = (P("dp", "mem"), P("dp"), P("dp"), P(), P(None, "mem"))
    return jax.shard_map(
        shards, mesh=mesh, in_specs=placed, out_specs=P(None, "mem"), check_vma=False
    )
```

profile of v0, /device:TPU:1, one launch (start us, length us, event | category | flops | bytes accessed | tf_op | source)
XLA Modules:
  0.0 980.9 jit_solution(6717442077956283194)
XLA Ops:
  6.5 2.0 convert_reduce_fusion
  8.6 23.6 %psum.49 = f32[3072]{0:T(1024)S(1)} all-reduce(f32[3072]{0:T(1024)S(1)} %convert_reduce_fusion), channel_id=1, replica_groups=mesh['dp'=32,'mem'=8] {'mem'}, use_global_device_ids=true, to_apply=%region_2.3 | all-reduce | flops 3072 | bytes 24576 | tf_op jit(solution)/shard_map/psum | solution.py:23
  33.7 2.6 fusion.1
  36.3 78.5 %all-gather.6.cloned.1.call-done = bf16[3072,2048]{1,0:T(8,128)(2,1)} async-done(((bf16[3072,256]{1,0:T(8,128)(2,1)}), bf16[3072,2048]{1,0:T(8,128)(2,1)}) %all-gather.6.cloned.1.call-update) | async-done | bytes 12582928 | tf_op jit(solution)/shard_map/all_gather | solution.py:41
  114.9 10.0 %fusion.12 = f32[2048,256]{1,0:T(8,128)} fusion(bf16[3072,2048]{1,0:T(8,128)(2,1)} %all-gather.6.cloned.1.call-done, bf16[3072,256]{1,0:T(8,128)(2,1)} %fusion.1), kind=kOutput, calls=%fused_computation.34 | convolution fusion | flops 3221225472 | bytes 16252928 | tf_op jit(solution)/shard_map/dot_general | solution.py:40
  125.0 211.7 %reduce-scatter.2.cloned.1.call-done = f32[64,256]{1,0:T(8,128)} async-done(((f32[2048,256]{1,0:T(8,128)}), f32[64,256]{1,0:T(8,128)}) %reduce-scatter.2.cloned.1.call-update) | async-done | bytes 65552 | tf_op jit(solution)/shard_map/reduce_scatter | solution.py:46
  338.2 79.4 %psum.50 = f32[]{:T(128)} all-reduce(f32[]{:T(128)} %fusion.4), channel_id=1, replica_groups=mesh['dp'=32,'mem'=8] {'dp','mem'}, use_global_device_ids=true, to_apply=%region_6.7 | all-reduce | flops 1 | bytes 8 | tf_op jit(solution)/shard_map/psum | solution.py:47
  418.2 1.5 add_divide_fusion
  419.9 13.6 %all_gather.28 = f32[64,2048]{1,0:T(8,128)S(1)} all-gather(f32[64,256]{1,0:T(8,128)S(1)} %compare_convert_fusion), channel_id=1, replica_groups=mesh['dp'=32,'mem'=8] {'mem'}, dimensions={1}, use_global_device_ids=true | all-gather | bytes 589824 | tf_op jit(solution)/shard_map/all_gather | solution.py:54
  433.5 57.2 %all-gather.8.cloned.1.call-done = f32[2048,256]{1,0:T(8,128)} async-done(((f32[64,256]{1,0:T(8,128)}), f32[2048,256]{1,0:T(8,128)}) %all-gather.8.cloned.1.call-update) | async-done | bytes 2097168 | tf_op jit(solution)/shard_map/all_gather | solution.py:58
  490.7 3.4 fusion.3
  494.2 17.9 %all_gather.33 = f32[64,2048]{1,0:T(8,128)S(1)} all-gather(f32[64,256]{1,0:T(8,128)S(1)} %copy-done.3), channel_id=1, replica_groups=mesh['dp'=32,'mem'=8] {'mem'}, dimensions={1}, use_global_device_ids=true | all-gather | bytes 589824 | tf_op jit(solution)/shard_map/all_gather | solution.py:53
  512.1 57.3 %all-gather.10.cloned.1.call-done = f32[2048,256]{1,0:T(8,128)} async-done(((f32[64,256]{1,0:T(8,128)}), f32[2048,256]{1,0:T(8,128)}) %all-gather.10.cloned.1.call-update) | async-done | bytes 2097168 | tf_op jit(solution)/shard_map/all_gather | solution.py:62
  569.4 3.5 fusion.14
  574.2 18.2 %all_gather.32 = f32[64,2048]{1,0:T(8,128)S(1)} all-gather(f32[64,256]{1,0:T(8,128)S(1)} %fusion.13), channel_id=1, replica_groups=mesh['dp'=32,'mem'=8] {'mem'}, dimensions={1}, use_global_device_ids=true | all-gather | bytes 589824 | tf_op jit(solution)/shard_map/all_gather | solution.py:54
  592.5 55.8 %all-gather.12.cloned.1.call-done = f32[2048,256]{1,0:T(8,128)} async-done(((f32[64,256]{1,0:T(8,128)}), f32[2048,256]{1,0:T(8,128)}) %all-gather.12.cloned.1.call-update) | async-done | bytes 2097168 | tf_op jit(solution)/shard_map/all_gather | solution.py:58
  648.3 3.4 fusion.2
  651.8 17.8 %all_gather.27 = f32[64,2048]{1,0:T(8,128)S(1)} all-gather(f32[64,256]{1,0:T(8,128)S(1)} %copy-done.4), channel_id=1, replica_groups=mesh['dp'=32,'mem'=8] {'mem'}, dimensions={1}, use_global_device_ids=true | all-gather | bytes 589824 | tf_op jit(solution)/shard_map/all_gather | solution.py:36
  670.4 58.6 %psum.51 = f32[256]{0:T(256)S(1)} all-reduce(f32[256]{0:T(256)S(1)} %bitcast.35), channel_id=1, replica_groups=mesh['dp'=32,'mem'=8] {'dp'}, use_global_device_ids=true, to_apply=%region_7.8 | all-reduce | flops 256 | bytes 2048 | tf_op jit(solution)/shard_map/psum | solution.py:30
  729.2 2.8 fusion.15
  732.1 25.7 %psum.52 = f32[64]{0:T(128)S(1)} all-reduce(f32[64]{0:T(128)S(1)} %convolution_bitcast_fusion.1), channel_id=1, replica_groups=mesh['dp'=32,'mem'=8] {'mem'}, use_global_device_ids=true, to_apply=%region_8.9 | all-reduce | flops 64 | bytes 512 | tf_op jit(solution)/shard_map/psum | solution.py:69
  758.0 55.7 %psum.53 = f32[256]{0:T(256)S(1)} all-reduce(f32[256]{0:T(256)S(1)} %bitcast.34), channel_id=1, replica_groups=mesh['dp'=32,'mem'=8] {'dp'}, use_global_device_ids=true, to_apply=%region_9.10 | all-reduce | flops 256 | bytes 2048 | tf_op jit(solution)/shard_map/psum | solution.py:72
  813.8 26.3 %psum.54 = f32[64]{0:T(128)S(1)} all-reduce(f32[64]{0:T(128)S(1)} %convolution_bitcast_fusion), channel_id=1, replica_groups=mesh['dp'=32,'mem'=8] {'mem'}, use_global_device_ids=true, to_apply=%region_10.11 | all-reduce | flops 64 | bytes 512 | tf_op jit(solution)/shard_map/psum | solution.py:74
  841.1 131.4 %all-reduce.2.cloned.1.call-done = f32[64,256]{1,0:T(8,128)} async-done(((f32[64,256]{1,0:T(8,128)}), f32[64,256]{1,0:T(8,128)}) %all-reduce.2.cloned.1.call-update) | async-done | bytes 65552 | tf_op jit(solution)/shard_map/psum | solution.py:72
  (43 shorter events, 8.6 us)
Async XLA Ops:
  6.5 27.1 %copy-start.2 = (bf16[3072,256]{1,0:T(8,128)(2,1)S(1)}, bf16[3072,256]{1,0:T(8,128)(2,1)}, u32[]{:S(2)}) copy-start(bf16[3072,256]{1,0:T(8,128)(2,1)} %param.5) | copy-start | bytes 4718596
  6.5 108.3 %all-gather.6.cloned.1.call-start = ((), (), s32[]{:S(2)}) async-start(), calls=%async_computation.1 | async-start | bytes 14155776 | tf_op jit(solution)/shard_map/all_gather | solution.py:41
  36.3 300.4 %reduce-scatter.2.cloned.1.call-start = ((), (), s32[]{:S(2)}) async-start(), calls=%async_computation.2 | async-start | bytes 2162688 | tf_op jit(solution)/shard_map/reduce_scatter | solution.py:46
  124.9 365.8 %all-gather.8.cloned.1.call-start = ((), (), s32[]{:S(2)}) async-start(), calls=%async_computation.3 | async-start | bytes 2162688 | tf_op jit(solution)/shard_map/all_gather | solution.py:58
  419.8 74.4 %copy-start.3 = (f32[64,256]{1,0:T(8,128)S(1)}, f32[64,256]{1,0:T(8,128)}, u32[]{:S(2)}) copy-start(f32[64,256]{1,0:T(8,128)} %add_divide_fusion) | copy-start | bytes 196612
  419.8 149.6 %all-gather.10.cloned.1.call-start = ((), (), s32[]{:S(2)}) async-start(), calls=%async_computation.4 | async-start | bytes 2162688 | tf_op jit(solution)/shard_map/all_gather | solution.py:62
  494.1 154.2 %all-gather.12.cloned.1.call-start = ((), (), s32[]{:S(2)}) async-start(), calls=%async_computation.5 | async-start | bytes 2162688 | tf_op jit(solution)/shard_map/all_gather | solution.py:58
  569.4 3.6 copy-start.1
  573.0 156.2 %all-gather.14.cloned.1.call-start = ((), (), s32[]{:S(2)}) async-start(), calls=%async_computation.6 | async-start | bytes 2162688 | tf_op jit(solution)/shard_map/all_gather | solution.py:62
  574.2 77.5 %copy-start.4 = (f32[64,256]{1,0:T(8,128)S(1)}, f32[64,256]{1,0:T(8,128)}, u32[]{:S(2)}) copy-start(f32[64,256]{1,0:T(8,128)} %param.9) | copy-start | bytes 196612
  574.2 95.5 %copy-start = (bf16[3072,256]{1,0:T(8,128)(2,1)S(1)}, bf16[3072,256]{1,0:T(8,128)(2,1)}, u32[]{:S(2)}) copy-start(bf16[3072,256]{1,0:T(8,128)(2,1)} %fusion.1) | copy-start | bytes 4718596
  651.7 320.8 %all-reduce.2.cloned.1.call-start = ((), (), s32[]{:S(2)}) async-start(), calls=%async_computation.7 | async-start | bytes 131072 | tf_op jit(solution)/shard_map/psum | solution.py:72
Sparse Core Ops, SparseCore 0:
  36.4 78.4 all-gather.5
  125.0 211.6 reduce-scatter.1
  419.9 70.7 all-gather.7
  494.2 75.1 all-gather.9
  573.1 75.1 all-gather.11
  651.8 75.2 all-gather.13
  841.2 131.2 all-reduce.1
where the time goes:
time: 985 us; the launch traced here: 981 us
  waiting for transfers between devices  592 us (60%)
  blocking collectives  337 us (34%)
  matrix products  26.3 us (3%)
  between operations  14.3 us (1%)
  other arithmetic  11.1 us (1%)
    reduce_scatter x1, waiting for transfers between devices, shards(): gram = lax.psum_scatter(strip, 'dp', scatter_dimension=0, tiled=True)  212 us
    psum x1, waiting for transfers between devices, shards(): moved, shares = lax.psum((moved_part, share_part), 'dp')  131 us
    all_gather x2, waiting for transfers between devices, shards(): lax.all_gather(current, 'dp', axis=0, tiled=True)  113 us
    psum x1, blocking collectives, shards(): total = lax.psum(jnp.sum(gram * identity), ('dp', 'mem'))  79.4 us
    all_gather x1, waiting for transfers between devices, shards(): lax.all_gather(decorrelated_lines, 'mem', axis=1, tiled=True)  78.5 us
    psum x1, blocking collectives, shards(): lax.psum(jnp.dot(innovation, decorrelated_lines.astype(jnp.float32), prec...  58.6 us
    all_gather x2, waiting for transfers between devices, shards(): piece = lax.all_gather(update, 'dp', axis=0, tiled=True)  57.3 us
    psum x1, blocking collectives, shards(): moved, shares = lax.psum((moved_part, share_part), 'dp')  55.7 us
  transfers between devices with their start and end apart: 7, of which 6 were waited for; matrix products, arithmetic and copies ran while one was open for 0% of the time, Pallas kernels for 0%

commit v1 on v0

v1 whole, which is shorter than its diff:
```python
import functools
import math

import jax
import jax.numpy as jnp
from jax import lax
from jax.experimental import pallas as pl
from jax.experimental.pallas import tpu as pltpu
from jax.sharding import PartitionSpec as P

MESH = pl.DeviceIdType.MESH
HIGHEST = lax.Precision.HIGHEST
NX, NY, NZ, NM = 4, 4, 8, 8
MEMBERS = 2048
CM = 256
NS = 3072
HALF = NS // 2
KT = 512
CHUNKS = (64, 64, 64, 32, 32)
STARTS = tuple(sum(CHUNKS[:i]) for i in range(len(CHUNKS)))
ROWS = (CM,) + tuple(2 * part for part in CHUNKS)
N_SEMS = 7 + 7 + 1 + 3 * len(CHUNKS) + 17 + 20 * len(ROWS) + 28 + 10
NT = (((1,), (1,)), ((), ()))


def piece(rows, index):
    groups = rows // 4 // 8
    lanes = NZ // groups
    width = 512 // lanes
    return (
        pl.ds(pl.multiple_of((index // lanes) * 8, 8), 8),
        pl.ds(pl.multiple_of((index % lanes) * width, 128), width),
    )


def piece_shape(rows):
    return (8, 512 // (NZ // (rows // 4 // 8)))


def kernel(var_ref, m_ref, obs_ref, cls_ref, ens_ref, out_ref, *scratch):
    (
        raw, relay, near, far, sib, white, sums, scale, bases, ensemble_in, centers,
        small, small_y, small_z, small_m, strip, vec, polys, exchange, rows_out, sems,
    ) = scratch[:21]
    lists = scratch[21:]
    n = len(ROWS)
    part, from_y, sum_y, from_z, gather_z = (lists[i * n : (i + 1) * n] for i in range(5))

    dp, mem = lax.axis_index("dp"), lax.axis_index("mem")
    z, y = dp // NY, dp % NY
    c, k = mem // 2, mem % 2

    def mem_at(offset):
        return (dp, (mem + offset) % NM)

    def x_at(offset):
        return (dp, ((c + offset + NX) % NX) * 2 + k)

    def y_at(offset):
        return (z * NY + (y + offset) % NY, mem)

    def z_at(offset):
        return (((z + offset) % NZ) * NY + y, mem)

    used = [0]
    pending = []

    def remote(src, dst, device):
        i = used[0]
        used[0] += 1
        return pltpu.make_async_remote_copy(
            src_ref=src,
            dst_ref=dst,
            send_sem=sems.at[0, i],
            recv_sem=sems.at[1, i],
            device_id=device,
            device_id_type=MESH,
        )

    def start(copies):
        for copy in copies:
            copy.start()
            pending.append(copy)

    def arrive(copies):
        for copy in copies:
            copy.wait_recv()

    def drain():
        while pending:
            pending.pop(0).wait_send()

    barrier = pltpu.get_barrier_semaphore()
    greeted = (
        [mem_at(j) for j in range(1, NM)]
        + [y_at(j) for j in range(1, NY)]
        + [z_at(j) for j in range(1, NZ)]
    )
    for device in greeted:
        pl.semaphore_signal(barrier, inc=1, device_id=device, device_id_type=MESH)

    eye = (
        lax.broadcasted_iota(jnp.int32, (CM, CM), 0) == lax.broadcasted_iota(jnp.int32, (CM, CM), 1)
    )
    turn = jnp.concatenate(
        [jnp.where(eye, 1.0, 0.0), jnp.ones((16, CM), jnp.float32)], axis=0
    ).astype(jnp.bfloat16)

    @pl.loop(0, NS // KT)
    def _(i):
        at = pl.ds(pl.multiple_of(i * KT, KT), KT)
        turned = lax.dot_general(turn, m_ref[at, :], NT, preferred_element_type=jnp.float32)
        raw[:, at] = turned[:CM].astype(jnp.bfloat16)
        bases[:, at] = turned[CM : CM + 1]

    sums[mem] = bases[...]
    group = pl.ds(pl.multiple_of(z * 8, 8), 8)
    ensemble_in[mem] = ens_ref[group, :]

    pl.semaphore_wait(barrier, len(greeted))

    sum_copies = [remote(sums.at[mem], sums.at[mem], mem_at(j)) for j in range(1, NM)]
    start(sum_copies)
    sib_copy = remote(raw, sib, (dp, mem + 1 - 2 * k))
    start([sib_copy])
    near_copies, relay_copies, far_copies = [], [], []
    half_of_far = pl.multiple_of((1 - c // 2) * HALF, HALF)
    for first, count in zip(STARTS, CHUNKS, strict=True):
        at = pl.ds(first, count)
        near_copies.append(remote(raw.at[at], near.at[at], x_at(-1)))
        relay_copies.append(remote(raw.at[at, pl.ds(half_of_far, HALF)], relay.at[at], x_at(1)))
        far_copies.append(remote(relay.at[at], far.at[at], x_at(1)))
    for i in range(2):
        start([near_copies[i], relay_copies[i]])
    ens_copies = [
        remote(ens_ref.at[group], ensemble_in.at[mem], mem_at(j)) for j in range(1, NM)
    ]
    start(ens_copies)

    classes = cls_ref[...]
    variance = jnp.zeros((1, NS), jnp.float32)
    for level in range(8):
        variance = jnp.where(classes == level, var_ref[level], variance)
    weight = lax.rsqrt(variance)
    scale[...] = weight / math.sqrt(MEMBERS - 1)

    arrive(sum_copies)
    total = sums[0]
    for j in range(1, NM):
        total = total + sums[j]
    average = total / MEMBERS
    bases[...] = average
    innovation = weight * (obs_ref[...] - average)

    def whiten(block, at):
        return (
            (block.astype(jnp.float32) - bases[:, at]) * scale[:, at]
        ).astype(jnp.bfloat16)

    own = pl.ds(pl.multiple_of(k * CM, CM), CM)
    other = pl.ds(pl.multiple_of((1 - k) * CM, CM), CM)
    for i in range(NS // KT):
        at = pl.ds(i * KT, KT)
        white[own, at] = whiten(raw[:, at], at)
    arrive([sib_copy])
    part[0][...] = jnp.zeros((CM, 512), jnp.float32)

    @pl.loop(0, NS // KT)
    def _(i):
        at = pl.ds(pl.multiple_of(i * KT, KT), KT)
        white[other, at] = whiten(sib[:, at], at)
        part[0][...] += lax.dot_general(
            white[own, at], white[:, at], NT, preferred_element_type=jnp.float32
        )

    def reduce_y(q):
        quarter = ROWS[q] // 4
        copies = []
        for j in range(1, NY):
            target = (y + j) % NY
            rows = pl.ds(pl.multiple_of(target * quarter, 8), quarter)
            copies.append(remote(part[q].at[rows], from_y[q].at[j - 1], y_at(j)))
        start(copies)
        return copies

    def reduce_z(q, copies):
        quarter = ROWS[q] // 4
        arrive(copies)
        mine = pl.ds(pl.multiple_of(y * quarter, 8), quarter)
        sum_y[q][...] = part[q][mine, :] + from_y[q][0] + from_y[q][1] + from_y[q][2]
        copies = []
        for j in range(1, NZ):
            rows, lanes = piece(ROWS[q], (z + j) % NZ)
            copies.append(remote(sum_y[q].at[rows, lanes], from_z[q].at[j - 1], z_at(j)))
        start(copies)
        return copies

    def spread_z(q, copies):
        arrive(copies)
        rows, lanes = piece(ROWS[q], z)
        total = sum_y[q][rows, lanes]
        for j in range(NZ - 1):
            total = total + from_z[q][j]
        gather_z[q][rows, lanes] = total
        here = gather_z[q].at[rows, lanes]
        copies = [remote(here, here, z_at(j)) for j in range(1, NZ)]
        start(copies)
        return copies

    def spread_y(q, copies):
        quarter = ROWS[q] // 4
        arrive(copies)
        if q == 0:
            first = y * quarter
        else:
            first = CM + (y // 2) * CM + STARTS[q - 1] + (y % 2) * quarter
        rows = pl.ds(pl.multiple_of(first, 8), quarter)
        strip[rows, :] = gather_z[q][...]
        copies = [remote(gather_z[q], strip.at[rows], y_at(j)) for j in range(1, NY)]
        start(copies)
        return copies

    half = pl.multiple_of((c // 2) * HALF, HALF)

    def gram_part(q):
        i = q - 1
        first, count = STARTS[i], CHUNKS[i]
        at_rows = pl.ds(first, count)
        arrive([near_copies[i]])
        if i + 1 < len(CHUNKS):
            arrive([relay_copies[i + 1]])
            start([far_copies[i + 1]])
        if i + 2 < len(CHUNKS):
            start([near_copies[i + 2], relay_copies[i + 2]])
        part[q][...] = jnp.zeros((2 * count, 512), jnp.float32)

        @pl.loop(0, NS // KT)
        def _(s):
            at = pl.ds(pl.multiple_of(s * KT, KT), KT)
            part[q][:count] += lax.dot_general(
                whiten(near[at_rows, at], at), white[:, at], NT, preferred_element_type=jnp.float32
            )

        arrive([far_copies[i]])

        @pl.loop(0, HALF // KT)
        def _(s):
            here = pl.ds(pl.multiple_of(s * KT, KT), KT)
            at = pl.ds(pl.multiple_of(half + s * KT, KT), KT)
            part[q][count:] += lax.dot_general(
                whiten(far[at_rows, here], at), white[:, at], NT, preferred_element_type=jnp.float32
            )

    stages = [reduce_z, spread_z, spread_y, lambda q, copies: arrive(copies)]
    state = {0: reduce_y(0)}
    arrive([relay_copies[0]])
    start([far_copies[0]])

    high = innovation.astype(jnp.bfloat16)
    rest = innovation - high.astype(jnp.float32)
    middle = rest.astype(jnp.bfloat16)
    low = (rest - middle.astype(jnp.float32)).astype(jnp.bfloat16)
    split = jnp.concatenate(
        [
            high.astype(jnp.float32),
            middle.astype(jnp.float32),
            low.astype(jnp.float32),
            jnp.zeros((13, NS), jnp.float32),
        ],
        axis=0,
    ).astype(jnp.bfloat16)
    shadow = lax.dot_general(split, white[own, :], NT, preferred_element_type=jnp.float32)
    diagonal = jnp.sum(
        jnp.where(eye, part[0][:, pl.ds(pl.multiple_of(k * CM, CM), CM)], 0.0), axis=0, keepdims=True
    )
    small[...] = jnp.concatenate(
        [jnp.sum(shadow[:8], axis=0, keepdims=True), diagonal, jnp.zeros((6, CM), jnp.float32)], axis=0
    )
    small_copies = [remote(small, small_y.at[j - 1], y_at(j)) for j in range(1, NY)]
    start(small_copies)

    def small_sum_y():
        arrive(small_copies)
        small_z[NZ - 1] = small[...] + small_y[0] + small_y[1] + small_y[2]
        copies = [remote(small_z.at[NZ - 1], small_z.at[j - 1], z_at(j)) for j in range(1, NZ)]
        start(copies)
        return copies

    def small_sum_z(copies):
        arrive(copies)
        total = small_z[0]
        for j in range(1, NZ):
            total = total + small_z[j]
        small_m[mem] = total
        copies = [remote(small_m.at[mem], small_m.at[mem], mem_at(j)) for j in range(1, NM)]
        start(copies)
        return copies

    def first_vectors(copies):
        arrive(ens_copies)
        arrive(copies)
        center = ensemble_in[0].sum(axis=1, keepdims=True)
        for j in range(1, NM):
            center = center + ensemble_in[j].sum(axis=1, keepdims=True)
        center = center / MEMBERS
        place = lax.broadcasted_iota(jnp.int32, (8, 1), 0)

        def own_rows(block):
            return [
                jnp.sum(jnp.where(place == 2 * y + i, block, 0.0), axis=0, keepdims=True)
                for i in range(2)
            ]

        centers[:2, :] = jnp.concatenate(own_rows(jnp.broadcast_to(center, (8, 128))), axis=0)
        for j in range(NM):
            vec[j] = jnp.concatenate(
                own_rows(ensemble_in[j] - center)
                + [small_m[j, 0:1, :], jnp.zeros((5, CM), jnp.float32)],
                axis=0,
            )

    small_state = None
    for t in range(1, n + len(stages)):
        for depth in range(len(stages), 0, -1):
            q = t - depth
            if 0 <= q < n:
                state[q] = stages[depth - 1](q, state[q])
        if t < n:
            gram_part(t)
            state[t] = reduce_y(t)
        if t == 1:
            small_state = small_sum_y()
        elif t == 2:
            small_state = small_sum_z(small_state)
        elif t == 3:
            first_vectors(small_state)

    trace = small_m[0, 1:2, :]
    for j in range(1, NM):
        trace = trace + small_m[j, 1:2, :]
    norm = (MEMBERS + jnp.sum(trace, axis=1, keepdims=True)) / MEMBERS

    next_one = ((c + 1) % NX) * 2 + k
    next_two = ((c + 2) % NX) * 2 + k

    def times(step):
        lhs = jnp.concatenate([vec[mem], vec[next_one], vec[next_two]], axis=1)
        exchange[step, mem, :, :512] = jnp.dot(
            lhs, strip[...], precision=HIGHEST, preferred_element_type=jnp.float32
        )
        lhs = jnp.concatenate([vec[2 * c], vec[2 * c + 1]], axis=1)
        exchange[step, mem, :, 512:] = lax.dot_general(
            lhs, strip[CM:, :], NT, precision=HIGHEST, preferred_element_type=jnp.float32
        )
        here = exchange.at[step, mem]
        copies = [remote(here, here, mem_at(j)) for j in range(1, NM)]
        start(copies)
        arrive(copies)
        result = []
        for chip in range(NX):
            for core in range(2):
                cols = slice(core * CM, (core + 1) * CM)
                product = (
                    exchange[step, 2 * chip, :, cols]
                    + exchange[step, 2 * chip + 1, :, cols]
                    + exchange[step, 2 * ((chip - 1) % NX) + core, :, 512:768]
                    + exchange[step, 2 * ((chip - 2) % NX) + core, :, 768:]
                )
                result.append((product + vec[2 * chip + core]) / norm)
        return result

    moved = times(0)
    for j in range(NM):
        vec[j] = 1.5 * vec[j] - 0.5 * moved[j]
        polys[j] = vec[j]
    moved = times(1)
    for j in range(NM):
        vec[j] = 1.5 * vec[j] - 0.5 * moved[j]
    moved = times(2)
    for j in range(NM):
        vec[j] = moved[j]
    moved = times(3)
    shift = jnp.zeros((2, 1), jnp.float32)
    for j in range(NM):
        applied = 1.5 * polys[j] - 0.5 * (1.5 * vec[j] - 0.5 * moved[j])
        polys[j] = applied
        shift = shift + jnp.sum(applied[:2] * applied[2:3], axis=1, keepdims=True)
    shift = shift / norm / math.sqrt(MEMBERS - 1)
    center = centers[:2, :1]
    rows_out[y, :2, :] = center + shift + polys[mem][:2] / jnp.sqrt(norm)
    here = rows_out.at[y]
    copies = [remote(here, here, y_at(j)) for j in range(1, NY)]
    start(copies)
    arrive(copies)
    out_ref[group, :] = jnp.concatenate([rows_out[j, :2, :] for j in range(NY)], axis=0)
    here = out_ref.at[group]
    copies = [remote(here, here, z_at(j)) for j in range(1, NZ)]
    start(copies)
    arrive(copies)
    drain()


def shards(modelled_reactions, observations, noise_class, class_variance, ensemble):
    f32, bf16 = jnp.float32, jnp.bfloat16
    vmem = pl.BlockSpec(memory_space=pltpu.VMEM)
    scratch = [
        pltpu.VMEM((CM, NS), bf16),
        pltpu.VMEM((CM, HALF), bf16),
        pltpu.VMEM((CM, NS), bf16),
        pltpu.VMEM((CM, HALF), bf16),
        pltpu.VMEM((CM, NS), bf16),
        pltpu.VMEM((2 * CM, NS), bf16),
        pltpu.VMEM((NM, 1, NS), f32),
        pltpu.VMEM((1, NS), f32),
        pltpu.VMEM((1, NS), f32),
        pltpu.VMEM((NM, 8, CM), f32),
        pltpu.VMEM((8, 128), f32),
        pltpu.VMEM((8, CM), f32),
        pltpu.VMEM((NY - 1, 8, CM), f32),
        pltpu.VMEM((NZ, 8, CM), f32),
        pltpu.VMEM((NM, 8, CM), f32),
        pltpu.VMEM((3 * CM, 512), f32),
        pltpu.VMEM((NM, 8, CM), f32),
        pltpu.VMEM((NM, 8, CM), f32),
        pltpu.VMEM((4, NM, 8, 1024), f32),
        pltpu.VMEM((NY, 8, CM), f32),
        pltpu.SemaphoreType.DMA((2, N_SEMS)),
    ]
    scratch += [pltpu.VMEM((r, 512), f32) for r in ROWS]
    scratch += [pltpu.VMEM((NY - 1, r // 4, 512), f32) for r in ROWS]
    scratch += [pltpu.VMEM((r // 4, 512), f32) for r in ROWS]
    scratch += [pltpu.VMEM((NZ - 1,) + piece_shape(r), f32) for r in ROWS]
    scratch += [pltpu.VMEM((r // 4, 512), f32) for r in ROWS]
    return pl.pallas_call(
        kernel,
        out_shape=jax.ShapeDtypeStruct((64, CM), f32),
        in_specs=[pl.BlockSpec(memory_space=pltpu.SMEM), vmem, vmem, vmem, vmem],
        out_specs=vmem,
        scratch_shapes=scratch,
        compiler_params=pltpu.CompilerParams(
            collective_id=0, has_side_effects=True, vmem_limit_bytes=40 * 1024 * 1024
        ),
    )(
        class_variance,
        modelled_reactions,
        observations.reshape(1, NS),
        noise_class.reshape(1, NS),
        ensemble,
    )


def solution(mesh):
    placed = (P("dp", "mem"), P("dp"), P("dp"), P(), P(None, "mem"))
    return jax.shard_map(
        shards, mesh=mesh, in_specs=placed, out_specs=P(None, "mem"), check_vma=False
    )
```

time: 985 us -> 123 us (0.12)
  waiting for transfers between devices: 592 us -> 0 us
  blocking collectives: 337 us -> 0 us
  Pallas kernels: 0 us -> 117 us
  matrix products: 26.3 us -> 0 us
  between operations: 14.3 us -> 0.01 us
  other arithmetic: 11.1 us -> 0 us
    psum x6 -> x0, blocking collectives: 269 us -> none  [the longest x1 79.4 us: shards(): total = lax.psum(jnp.sum(gram * identity), ('dp', 'mem'))]
    all_gather x5 -> x0, waiting for transfers between devices: 249 us -> none  [the longest x2 113 us: shards(): lax.all_gather(current, 'dp', axis=0, tiled=True)]
    reduce_scatter x1 -> x0, waiting for transfers between devices: 212 us -> none  [shards(): gram = lax.psum_scatter(strip, 'dp', scatter_dimension=0, tiled=True)]
    psum x1 -> x0, waiting for transfers between devices: 131 us -> none  [shards(): moved, shares = lax.psum((moved_part, share_part), 'dp')]
    pallas_call x0 -> x1, Pallas kernels: none -> 117 us  [shards(): pl.pallas_call(kernel, out_shape=jax.ShapeDtypeStruct((64, CM), f32), in_...]
    all_gather x4 -> x0, blocking collectives: 67.6 us -> none  [the longest x2 31.8 us: shards(): lax.all_gather(inverse, 'mem', axis=1, tiled=True)]
    dot_general x11 -> x0, matrix products: 26.3 us -> none  [the longest x1 10 us: shards(): lax.dot_general(lax.all_gather(decorrelated_lines, 'mem', axis=1, tiled=T...]
  transfers between devices with their start and end apart: 7 -> 0, of which waited for: 6 -> 0; matrix products, arithmetic and copies ran while one was open for 0% -> 0% of each run, Pallas kernels for 0% -> 0%
where the time goes in v1:
time: 123 us; the launch traced here: 122 us
  Pallas kernels  117 us (95%)
  local copies, waits for them, and re-layouts  4.95 us (4%)
    pallas_call x1, Pallas kernels, shards(): pl.pallas_call(kernel, out_shape=jax.ShapeDtypeStruct((64, CM), f32), in_...  117 us
    unnamed x11, local copies, waits for them, and re-layouts  4.95 us

profile of v1, /device:TPU:1, one launch (start us, length us, event | category | flops | bytes accessed | tf_op | source)
XLA Modules:
  0.0 122.3 jit_solution(4898722189929973785)
XLA Ops:
  0.0 0.0 copy-start
  0.0 1.4 %copy-done = bf16[3072,256]{1,0:T(8,128)(2,1)S(1)} copy-done((bf16[3072,256]{1,0:T(8,128)(2,1)S(1)}, bf16[3072,256]{1,0:T(8,128)(2,1)}, u32[]{:S(2)}) %copy-start) | copy-done | bytes 1572888
  1.4 0.0 copy-start.1
  1.4 0.8 copy-done.1
  2.2 0.0 copy-start.2
  2.3 0.7 copy-done.2
  3.0 0.0 copy-start.3
  3.0 0.7 copy-done.3
  3.7 0.0 copy-start.4
  3.7 0.7 copy-done.4
  4.3 117.3 %shard_map.55 = f32[64,256]{1,0:T(8,128)S(1)} custom-call(f32[8]{0:T(128)S(1)} %copy-done.4, bf16[3072,256]{1,0:T(8,128)(2,1)S(1)} %copy-done, f32[1,3072]{1,0:T(1,128)S(1)} %bitcast.2, s32[1,3072]{1,0:T(1,128)S(1)} %bitcast.3, f32[64,256]{1,0:T(8,128)S(1)} %copy-done.1), custom_call_target="tpu_custom_call" | custom-call | tf_op jit(solution)/shard_map/pallas_call | solution.py:434
  121.6 0.6 copy.7
Async XLA Ops:
  0.0 1.4 %copy-start = (bf16[3072,256]{1,0:T(8,128)(2,1)S(1)}, bf16[3072,256]{1,0:T(8,128)(2,1)}, u32[]{:S(2)}) copy-start(bf16[3072,256]{1,0:T(8,128)(2,1)} %m_ref.1) | copy-start | bytes 4718596
  1.4 0.8 copy-start.1
  2.2 0.7 copy-start.2
  3.0 0.7 copy-start.3
  3.7 0.7 copy-start.4

commit v2 on v1

--- a/solution.py
+++ b/solution.py
@@ -1,4 +1,3 @@
-import functools
 import math
 
 import jax
@@ -9,17 +8,20 @@
 from jax.sharding import PartitionSpec as P
 
 MESH = pl.DeviceIdType.MESH
-HIGHEST = lax.Precision.HIGHEST
 NX, NY, NZ, NM = 4, 4, 8, 8
 MEMBERS = 2048
 CM = 256
 NS = 3072
 HALF = NS // 2
 KT = 512
-CHUNKS = (64, 64, 64, 32, 32)
+CHUNKS = (128, 64, 32, 32)
 STARTS = tuple(sum(CHUNKS[:i]) for i in range(len(CHUNKS)))
 ROWS = (CM,) + tuple(2 * part for part in CHUNKS)
-N_SEMS = 7 + 7 + 1 + 3 * len(CHUNKS) + 17 + 20 * len(ROWS) + 28 + 10
+PREV = 2
+VR = 4
+WIDE = 5 * CM
+N_SEMS = 7 + 7 + 1 + len(CHUNKS) + 2 * PREV + 17 + 20 * len(ROWS) + 28 + 10
+N_LOADS = NS // KT + 4
 NT = (((1,), (1,)), ((), ()))
 
 
@@ -37,12 +39,28 @@
     return (8, 512 // (NZ // (rows // 4 // 8)))
 
 
-def kernel(var_ref, m_ref, obs_ref, cls_ref, ens_ref, out_ref, *scratch):
+def split_in_three(value):
+    high = value.astype(jnp.bfloat16)
+    rest = value - high.astype(jnp.float32)
+    middle = rest.astype(jnp.bfloat16)
+    return high, middle, (rest - middle.astype(jnp.float32)).astype(jnp.bfloat16)
+
+
+def stacked(value, rows):
+    terms = [term.astype(jnp.float32) for term in split_in_three(value)]
+    spare = rows - 3 * value.shape[0]
+    return jnp.concatenate(
+        terms + [jnp.zeros((spare, value.shape[1]), jnp.float32)], axis=0
+    ).astype(jnp.bfloat16)
+
+
+def kernel(var_hbm, m_hbm, obs_hbm, cls_hbm, ens_hbm, out_ref, *scratch):
     (
-        raw, relay, near, far, sib, white, sums, scale, bases, ensemble_in, centers,
-        small, small_y, small_z, small_m, strip, vec, polys, exchange, rows_out, sems,
-    ) = scratch[:21]
-    lists = scratch[21:]
+        m_ref, obs_ref, cls_ref, var_ref, raw, near, prev, sib, white, white_prev, sums, scale, bases,
+        ensemble_in, centers, small, small_y, small_z, small_m, strip, terms, vec, polys, exchange,
+        rows_out, loads, sems,
+    ) = scratch[:27]
+    lists = scratch[27:]
     n = len(ROWS)
     part, from_y, sum_y, from_z, gather_z = (lists[i * n : (i + 1) * n] for i in range(5))
 
@@ -62,6 +80,7 @@
     def z_at(offset):
         return (((z + offset) % NZ) * NY + y, mem)
 
+    sibling = (dp, mem + 1 - 2 * k)
     used = [0]
     pending = []
 
@@ -90,6 +109,21 @@
         while pending:
             pending.pop(0).wait_send()
 
+    group = pl.ds(pl.multiple_of(z * 8, 8), 8)
+    fetches = []
+    for i in range(NS // KT):
+        at = pl.ds(i * KT, KT)
+        fetches.append(pltpu.make_async_copy(m_hbm.at[at], m_ref.at[at], loads.at[i]))
+    for src, dst in (
+        (cls_hbm, cls_ref),
+        (obs_hbm, obs_ref),
+        (var_hbm, var_ref),
+        (ens_hbm.at[group], ensemble_in.at[mem]),
+    ):
+        fetches.append(pltpu.make_async_copy(src, dst, loads.at[len(fetches)]))
+    for fetch in fetches:
+        fetch.start()
+
     barrier = pltpu.get_barrier_semaphore()
     greeted = (
         [mem_at(j) for j in range(1, NM)]
@@ -105,37 +139,44 @@
     turn = jnp.concatenate(
         [jnp.where(eye, 1.0, 0.0), jnp.ones((16, CM), jnp.float32)], axis=0
     ).astype(jnp.bfloat16)
-
-    @pl.loop(0, NS // KT)
-    def _(i):
-        at = pl.ds(pl.multiple_of(i * KT, KT), KT)
+    for i in range(NS // KT):
+        at = pl.ds(i * KT, KT)
+        fetches[i].wait()
         turned = lax.dot_general(turn, m_ref[at, :], NT, preferred_element_type=jnp.float32)
         raw[:, at] = turned[:CM].astype(jnp.bfloat16)
-        bases[:, at] = turned[CM : CM + 1]
-
-    sums[mem] = bases[...]
-    group = pl.ds(pl.multiple_of(z * 8, 8), 8)
-    ensemble_in[mem] = ens_ref[group, :]
+        sums[mem, :, at] = turned[CM : CM + 1]
+    for fetch in fetches[NS // KT :]:
+        fetch.wait()
 
     pl.semaphore_wait(barrier, len(greeted))
 
+    own = pl.ds(pl.multiple_of(k * CM, CM), CM)
+    other = pl.ds(pl.multiple_of((1 - k) * CM, CM), CM)
     sum_copies = [remote(sums.at[mem], sums.at[mem], mem_at(j)) for j in range(1, NM)]
     start(sum_copies)
-    sib_copy = remote(raw, sib, (dp, mem + 1 - 2 * k))
+    ens_copies = [
+        remote(ensemble_in.at[mem], ensemble_in.at[mem], mem_at(j)) for j in range(1, NM)
+    ]
+    start(ens_copies)
+    sib_copy = remote(raw, sib, sibling)
     start([sib_copy])
-    near_copies, relay_copies, far_copies = [], [], []
-    half_of_far = pl.multiple_of((1 - c // 2) * HALF, HALF)
+    near_copies = []
     for first, count in zip(STARTS, CHUNKS, strict=True):
         at = pl.ds(first, count)
         near_copies.append(remote(raw.at[at], near.at[at], x_at(-1)))
-        relay_copies.append(remote(raw.at[at, pl.ds(half_of_far, HALF)], relay.at[at], x_at(1)))
-        far_copies.append(remote(relay.at[at], far.at[at], x_at(1)))
-    for i in range(2):
-        start([near_copies[i], relay_copies[i]])
-    ens_copies = [
-        remote(ens_ref.at[group], ensemble_in.at[mem], mem_at(j)) for j in range(1, NM)
-    ]
-    start(ens_copies)
+    next_half = pl.multiple_of((((c + 1) % NX) // 2) * HALF, HALF)
+    prev_copies, shared_copies = [], []
+    for i in range(PREV):
+        rows = CM // PREV
+        to_rows = pl.ds(pl.multiple_of(k * CM + i * rows, rows), rows)
+        prev_copies.append(
+            remote(
+                raw.at[pl.ds(i * rows, rows), pl.ds(next_half, HALF)], prev.at[to_rows], x_at(1)
+            )
+        )
+        shared_copies.append(remote(prev.at[to_rows], prev.at[to_rows], sibling))
+    start(near_copies)
+    start(prev_copies)
 
     classes = cls_ref[...]
     variance = jnp.zeros((1, NS), jnp.float32)
@@ -153,12 +194,8 @@
     innovation = weight * (obs_ref[...] - average)
 
     def whiten(block, at):
-        return (
-            (block.astype(jnp.float32) - bases[:, at]) * scale[:, at]
-        ).astype(jnp.bfloat16)
-
-    own = pl.ds(pl.multiple_of(k * CM, CM), CM)
-    other = pl.ds(pl.multiple_of((1 - k) * CM, CM), CM)
+        return ((block.astype(jnp.float32) - bases[:, at]) * scale[:, at]).astype(jnp.bfloat16)
+
     for i in range(NS // KT):
         at = pl.ds(i * KT, KT)
         white[own, at] = whiten(raw[:, at], at)
@@ -220,6 +257,17 @@
         start(copies)
         return copies
 
+    def finish(q, copies):
+        arrive(copies)
+        if q == 0:
+            blocks = [(0, CM)]
+        else:
+            blocks = [(CM + STARTS[q - 1], CHUNKS[q - 1]), (2 * CM + STARTS[q - 1], CHUNKS[q - 1])]
+        for first, count in blocks:
+            at = pl.ds(first, count)
+            for i, term in enumerate(split_in_three(strip[at, :])):
+                terms[i, at, :] = term
+
     half = pl.multiple_of((c // 2) * HALF, HALF)
 
     def gram_part(q):
@@ -227,11 +275,6 @@
         first, count = STARTS[i], CHUNKS[i]
         at_rows = pl.ds(first, count)
         arrive([near_copies[i]])
-        if i + 1 < len(CHUNKS):
-            arrive([relay_copies[i + 1]])
-            start([far_copies[i + 1]])
-        if i + 2 < len(CHUNKS):
-            start([near_copies[i + 2], relay_copies[i + 2]])
         part[q][...] = jnp.zeros((2 * count, 512), jnp.float32)
 
         @pl.loop(0, NS // KT)
@@ -241,35 +284,21 @@
                 whiten(near[at_rows, at], at), white[:, at], NT, preferred_element_type=jnp.float32
             )
 
-        arrive([far_copies[i]])
-
         @pl.loop(0, HALF // KT)
         def _(s):
             here = pl.ds(pl.multiple_of(s * KT, KT), KT)
             at = pl.ds(pl.multiple_of(half + s * KT, KT), KT)
             part[q][count:] += lax.dot_general(
-                whiten(far[at_rows, here], at), white[:, at], NT, preferred_element_type=jnp.float32
-            )
-
-    stages = [reduce_z, spread_z, spread_y, lambda q, copies: arrive(copies)]
+                whiten(near[at_rows, at], at), white_prev[:, here], NT, preferred_element_type=jnp.float32
+            )
+
+        state[q] = reduce_y(q)
+
     state = {0: reduce_y(0)}
-    arrive([relay_copies[0]])
-    start([far_copies[0]])
-
-    high = innovation.astype(jnp.bfloat16)
-    rest = innovation - high.astype(jnp.float32)
-    middle = rest.astype(jnp.bfloat16)
-    low = (rest - middle.astype(jnp.float32)).astype(jnp.bfloat16)
-    split = jnp.concatenate(
-        [
-            high.astype(jnp.float32),
-            middle.astype(jnp.float32),
-            low.astype(jnp.float32),
-            jnp.zeros((13, NS), jnp.float32),
-        ],
-        axis=0,
-    ).astype(jnp.bfloat16)
-    shadow = lax.dot_general(split, white[own, :], NT, preferred_element_type=jnp.float32)
+
+    shadow = lax.dot_general(
+        stacked(innovation, 16), white[own, :], NT, preferred_element_type=jnp.float32
+    )
     diagonal = jnp.sum(
         jnp.where(eye, part[0][:, pl.ds(pl.multiple_of(k * CM, CM), CM)], 0.0), axis=0, keepdims=True
     )
@@ -279,8 +308,8 @@
     small_copies = [remote(small, small_y.at[j - 1], y_at(j)) for j in range(1, NY)]
     start(small_copies)
 
-    def small_sum_y():
-        arrive(small_copies)
+    def small_sum_y(copies):
+        arrive(copies)
         small_z[NZ - 1] = small[...] + small_y[0] + small_y[1] + small_y[2]
         copies = [remote(small_z.at[NZ - 1], small_z.at[j - 1], z_at(j)) for j in range(1, NZ)]
         start(copies)
@@ -315,43 +344,89 @@
         for j in range(NM):
             vec[j] = jnp.concatenate(
                 own_rows(ensemble_in[j] - center)
-                + [small_m[j, 0:1, :], jnp.zeros((5, CM), jnp.float32)],
+                + [small_m[j, 0:1, :], jnp.zeros((VR - 3, CM), jnp.float32)],
                 axis=0,
             )
 
-    small_state = None
-    for t in range(1, n + len(stages)):
-        for depth in range(len(stages), 0, -1):
-            q = t - depth
-            if 0 <= q < n:
-                state[q] = stages[depth - 1](q, state[q])
-        if t < n:
-            gram_part(t)
-            state[t] = reduce_y(t)
-        if t == 1:
-            small_state = small_sum_y()
-        elif t == 2:
-            small_state = small_sum_z(small_state)
-        elif t == 3:
-            first_vectors(small_state)
+    def advance(stage, q):
+        state[q] = stage(q, state[q])
+
+    def share_prev(i):
+        arrive([prev_copies[i]])
+        start([shared_copies[i]])
+
+    share_prev(0)
+    small_state = small_sum_y(small_copies)
+    advance(reduce_z, 0)
+    small_state = small_sum_z(small_state)
+    share_prev(1)
+    arrive(shared_copies)
+
+    @pl.loop(0, HALF // KT)
+    def _(s):
+        here = pl.ds(pl.multiple_of(s * KT, KT), KT)
+        at = pl.ds(pl.multiple_of(half + s * KT, KT), KT)
+        white_prev[:, here] = whiten(prev[:, here], at)
+
+    gram_part(1)
+    advance(spread_z, 0)
+    gram_part(2)
+    advance(reduce_z, 1)
+    advance(spread_y, 0)
+    gram_part(3)
+    advance(spread_z, 1)
+    advance(reduce_z, 2)
+    gram_part(4)
+    advance(reduce_z, 3)
+    advance(spread_y, 1)
+    advance(spread_z, 2)
+    advance(finish, 0)
+    advance(reduce_z, 4)
+    advance(spread_z, 3)
+    advance(spread_y, 2)
+    advance(spread_z, 4)
+    advance(spread_y, 3)
+    first_vectors(small_state)
+    advance(finish, 1)
+    advance(spread_y, 4)
+    advance(finish, 2)
+    advance(finish, 3)
+    advance(finish, 4)
 
     trace = small_m[0, 1:2, :]
     for j in range(1, NM):
         trace = trace + small_m[j, 1:2, :]
     norm = (MEMBERS + jnp.sum(trace, axis=1, keepdims=True)) / MEMBERS
 
-    next_one = ((c + 1) % NX) * 2 + k
-    next_two = ((c + 2) % NX) * 2 + k
+    def folded(rows):
+        return rows[:VR] + rows[VR : 2 * VR] + rows[2 * VR : 3 * VR]
 
     def times(step):
-        lhs = jnp.concatenate([vec[mem], vec[next_one], vec[next_two]], axis=1)
-        exchange[step, mem, :, :512] = jnp.dot(
-            lhs, strip[...], precision=HIGHEST, preferred_element_type=jnp.float32
-        )
-        lhs = jnp.concatenate([vec[2 * c], vec[2 * c + 1]], axis=1)
-        exchange[step, mem, :, 512:] = lax.dot_general(
-            lhs, strip[CM:, :], NT, precision=HIGHEST, preferred_element_type=jnp.float32
-        )
+        ahead = vec[((c + 1) % NX) * 2 + k]
+        behind = ((c + NX - 1) % NX) * 2
+        down = stacked(jnp.concatenate([vec[mem], ahead], axis=1), 4 * VR)
+        across = stacked(jnp.concatenate([vec[2 * c], vec[2 * c + 1]], axis=1), 4 * VR)
+        back = stacked(jnp.concatenate([vec[behind], vec[behind + 1]], axis=1), 4 * VR)
+        for_next = for_own = for_last = 0.0
+        for i in range(3):
+            for_next = (
+                for_next
+                + lax.dot_general(
+                    across, terms[i, CM : 2 * CM, :], NT, preferred_element_type=jnp.float32
+                )
+                + lax.dot_general(
+                    back, terms[i, 2 * CM :, :], NT, preferred_element_type=jnp.float32
+                )
+            )
+            for_own = for_own + jnp.dot(
+                down, terms[i, : 2 * CM, :], preferred_element_type=jnp.float32
+            )
+            for_last = for_last + jnp.dot(
+                down[:, CM:], terms[i, 2 * CM :, :], preferred_element_type=jnp.float32
+            )
+        exchange[step, mem, :, :CM] = folded(for_next)
+        exchange[step, mem, :, CM : 3 * CM] = folded(for_own)
+        exchange[step, mem, :, 3 * CM :] = folded(for_last)
         here = exchange.at[step, mem]
         copies = [remote(here, here, mem_at(j)) for j in range(1, NM)]
         start(copies)
@@ -359,12 +434,15 @@
         result = []
         for chip in range(NX):
             for core in range(2):
-                cols = slice(core * CM, (core + 1) * CM)
+                mine = slice((core + 1) * CM, (core + 2) * CM)
+                last = slice((core + 3) * CM, (core + 4) * CM)
+                above = 2 * ((chip + 1) % NX)
                 product = (
-                    exchange[step, 2 * chip, :, cols]
-                    + exchange[step, 2 * chip + 1, :, cols]
-                    + exchange[step, 2 * ((chip - 1) % NX) + core, :, 512:768]
-                    + exchange[step, 2 * ((chip - 2) % NX) + core, :, 768:]
+                    exchange[step, 2 * ((chip - 1) % NX) + core, :, :CM]
+                    + exchange[step, 2 * chip, :, mine]
+                    + exchange[step, 2 * chip + 1, :, mine]
+                    + exchange[step, above, :, last]
+                    + exchange[step, above + 1, :, last]
                 )
                 result.append((product + vec[2 * chip + core]) / norm)
         return result
@@ -386,8 +464,7 @@
         polys[j] = applied
         shift = shift + jnp.sum(applied[:2] * applied[2:3], axis=1, keepdims=True)
     shift = shift / norm / math.sqrt(MEMBERS - 1)
-    center = centers[:2, :1]
-    rows_out[y, :2, :] = center + shift + polys[mem][:2] / jnp.sqrt(norm)
+    rows_out[y, :2, :] = centers[:2, :1] + shift + polys[mem][:2] / jnp.sqrt(norm)
     here = rows_out.at[y]
     copies = [remote(here, here, y_at(j)) for j in range(1, NY)]
     start(copies)
@@ -402,14 +479,18 @@
 
 def shards(modelled_reactions, observations, noise_class, class_variance, ensemble):
     f32, bf16 = jnp.float32, jnp.bfloat16
-    vmem = pl.BlockSpec(memory_space=pltpu.VMEM)
+    hbm = pl.BlockSpec(memory_space=pltpu.HBM)
     scratch = [
+        pltpu.VMEM((NS, CM), bf16),
+        pltpu.VMEM((1, NS), f32),
+        pltpu.VMEM((1, NS), jnp.int32),
+        pltpu.SMEM((8,), f32),
         pltpu.VMEM((CM, NS), bf16),
-        pltpu.VMEM((CM, HALF), bf16),
         pltpu.VMEM((CM, NS), bf16),
-        pltpu.VMEM((CM, HALF), bf16),
+        pltpu.VMEM((2 * CM, HALF), bf16),
         pltpu.VMEM((CM, NS), bf16),
         pltpu.VMEM((2 * CM, NS), bf16),
+        pltpu.VMEM((2 * CM, HALF), bf16),
         pltpu.VMEM((NM, 1, NS), f32),
         pltpu.VMEM((1, NS), f32),
         pltpu.VMEM((1, NS), f32),
@@ -420,10 +501,12 @@
         pltpu.VMEM((NZ, 8, CM), f32),
         pltpu.VMEM((NM, 8, CM), f32),
         pltpu.VMEM((3 * CM, 512), f32),
-        pltpu.VMEM((NM, 8, CM), f32),
-        pltpu.VMEM((NM, 8, CM), f32),
-        pltpu.VMEM((4, NM, 8, 1024), f32),
+        pltpu.VMEM((3, 3 * CM, 512), bf16),
+        pltpu.VMEM((NM, VR, CM), f32),
+        pltpu.VMEM((NM, VR, CM), f32),
+        pltpu.VMEM((4, NM, VR, WIDE), f32),
         pltpu.VMEM((NY, 8, CM), f32),
+        pltpu.SemaphoreType.DMA((N_LOADS,)),
         pltpu.SemaphoreType.DMA((2, N_SEMS)),
     ]
     scratch += [pltpu.VMEM((r, 512), f32) for r in ROWS]
@@ -434,8 +517,8 @@
     return pl.pallas_call(
         kernel,
         out_shape=jax.ShapeDtypeStruct((64, CM), f32),
-        in_specs=[pl.BlockSpec(memory_space=pltpu.SMEM), vmem, vmem, vmem, vmem],
-        out_specs=vmem,
+        in_specs=[hbm] * 5,
+        out_specs=pl.BlockSpec(memory_space=pltpu.VMEM),
         scratch_shapes=scratch,
         compiler_params=pltpu.CompilerParams(
             collective_id=0, has_side_effects=True, vmem_limit_bytes=40 * 1024 * 1024

time: 123 us -> 110 us (0.89)
  Pallas kernels: 117 us -> 105 us
    pallas_call x1, Pallas kernels: 117 us -> 105 us  [shards(): pl.pallas_call(kernel, out_shape=jax.ShapeDtypeStruct((64, CM), f32), in_...]
where the time goes in v2:
time: 110 us
  Pallas kernels  105 us (95%)
  local copies, waits for them, and re-layouts  4.95 us (4%)
    pallas_call x1, Pallas kernels, shards(): pl.pallas_call(kernel, out_shape=jax.ShapeDtypeStruct((64, CM), f32), in_...  105 us
    unnamed x11, local copies, waits for them, and re-layouts  4.95 us

profile of v2, /device:TPU:1, one launch (start us, length us, event | category | flops | bytes accessed | tf_op | source)
XLA Modules:
  0.0 109.6 jit_solution(476750280962825870)
XLA Ops:
  0.0 0.0 copy-start
  0.0 1.4 %copy-done = bf16[3072,256]{1,0:T(8,128)(2,1)S(1)} copy-done((bf16[3072,256]{1,0:T(8,128)(2,1)S(1)}, bf16[3072,256]{1,0:T(8,128)(2,1)}, u32[]{:S(2)}) %copy-start) | copy-done | bytes 1572888
  1.4 0.0 copy-start.1
  1.4 0.8 copy-done.1
  2.2 0.0 copy-start.2
  2.3 0.7 copy-done.2
  3.0 0.0 copy-start.3
  3.0 0.7 copy-done.3
  3.7 0.0 copy-start.4
  3.7 0.7 copy-done.4
  4.3 104.6 %shard_map.55 = f32[64,256]{1,0:T(8,128)S(1)} custom-call(f32[8]{0:T(128)S(1)} %copy-done.4, bf16[3072,256]{1,0:T(8,128)(2,1)S(1)} %copy-done, f32[1,3072]{1,0:T(1,128)S(1)} %bitcast.2, s32[1,3072]{1,0:T(1,128)S(1)} %bitcast.3, f32[64,256]{1,0:T(8,128)S(1)} %copy-done.1), custom_call_target="tpu_custom_call" | custom-call | tf_op jit(solution)/shard_map/pallas_call | solution.py:517
  109.0 0.6 copy.7
Async XLA Ops:
  0.0 1.4 %copy-start = (bf16[3072,256]{1,0:T(8,128)(2,1)S(1)}, bf16[3072,256]{1,0:T(8,128)(2,1)}, u32[]{:S(2)}) copy-start(bf16[3072,256]{1,0:T(8,128)(2,1)} %m_hbm.1) | copy-start | bytes 4718596
  1.4 0.8 copy-start.1
  2.2 0.7 copy-start.2
  3.0 0.7 copy-start.3
  3.7 0.7 copy-start.4

commit v3 on v2

--- a/solution.py
+++ b/solution.py
@@ -14,14 +14,31 @@
 NS = 3072
 HALF = NS // 2
 KT = 512
-CHUNKS = (128, 64, 32, 32)
+CHUNKS = (64, 64, 64, 32, 32)
 STARTS = tuple(sum(CHUNKS[:i]) for i in range(len(CHUNKS)))
-ROWS = (CM,) + tuple(2 * part for part in CHUNKS)
+PARTS = (
+    ((0,), 0, 128, 0),
+    ((0,), 128, 128, 0),
+    ((1,), 0, 64, 1),
+    ((1,), 64, 64, 2),
+    ((2,), 0, 128, 2),
+    ((1, 2), 128, 64, 3),
+    ((1, 2), 192, 32, 4),
+    ((1, 2), 224, 32, 5),
+)
+ROWS = tuple(len(blocks) * count for blocks, _, count, _ in PARTS)
+ORDER = (
+    (0, 0), (1, 0), "small", (2, 0), "prev 0", (2, 1), (0, 1), (1, 1), "prev 1", (3, 0), "white prev", (4, 0),
+    (2, 2), "small y", (3, 1), (1, 2), (5, 0), (0, 2), (4, 1), (3, 2), "small z", (1, 3), (6, 0), (5, 1), (7, 0),
+    (0, 3), (4, 2), (6, 1), (2, 3), (3, 3), (7, 1), (5, 2), (4, 3), (6, 2), (7, 2), (5, 3), (1, 4), (6, 3),
+    "vectors", (7, 3), (0, 4), (4, 4), (6, 4), (5, 4), (3, 4), (2, 4), (7, 4),
+)
 PREV = 2
 VR = 4
 WIDE = 5 * CM
 N_SEMS = 7 + 7 + 1 + len(CHUNKS) + 2 * PREV + 17 + 20 * len(ROWS) + 28 + 10
 N_LOADS = NS // KT + 4
+FAR_Z = (4, 3, 5, 2, 6, 1, 7)
 NT = (((1,), (1,)), ((), ()))
 
 
@@ -68,11 +85,14 @@
     z, y = dp // NY, dp % NY
     c, k = mem // 2, mem % 2
 
-    def mem_at(offset):
-        return (dp, (mem + offset) % NM)
-
     def x_at(offset):
         return (dp, ((c + offset + NX) % NX) * 2 + k)
+
+    others = [(2, 0), (2, 1), (1, 0), (-1, 0), (1, 1), (-1, 1), (0, 1)]
+
+    def mem_peer(j):
+        chips, cores = others[j - 1]
+        return (dp, ((c + chips + NX) % NX) * 2 + (k + cores) % 2)
 
     def y_at(offset):
         return (z * NY + (y + offset) % NY, mem)
@@ -126,7 +146,7 @@
 
     barrier = pltpu.get_barrier_semaphore()
     greeted = (
-        [mem_at(j) for j in range(1, NM)]
+        [mem_peer(j) for j in range(1, NM)]
         + [y_at(j) for j in range(1, NY)]
         + [z_at(j) for j in range(1, NZ)]
     )
@@ -152,10 +172,10 @@
 
     own = pl.ds(pl.multiple_of(k * CM, CM), CM)
     other = pl.ds(pl.multiple_of((1 - k) * CM, CM), CM)
-    sum_copies = [remote(sums.at[mem], sums.at[mem], mem_at(j)) for j in range(1, NM)]
+    sum_copies = [remote(sums.at[mem], sums.at[mem], mem_peer(j)) for j in range(1, NM)]
     start(sum_copies)
     ens_copies = [
-        remote(ensemble_in.at[mem], ensemble_in.at[mem], mem_at(j)) for j in range(1, NM)
+        remote(ensemble_in.at[mem], ensemble_in.at[mem], mem_peer(j)) for j in range(1, NM)
     ]
     start(ens_copies)
     sib_copy = remote(raw, sib, sibling)
@@ -200,17 +220,14 @@
         at = pl.ds(i * KT, KT)
         white[own, at] = whiten(raw[:, at], at)
     arrive([sib_copy])
-    part[0][...] = jnp.zeros((CM, 512), jnp.float32)
 
     @pl.loop(0, NS // KT)
     def _(i):
         at = pl.ds(pl.multiple_of(i * KT, KT), KT)
         white[other, at] = whiten(sib[:, at], at)
-        part[0][...] += lax.dot_general(
-            white[own, at], white[:, at], NT, preferred_element_type=jnp.float32
-        )
-
-    def reduce_y(q):
+
+    def reduce_y(q, _):
+        gram_part(q)
         quarter = ROWS[q] // 4
         copies = []
         for j in range(1, NY):
@@ -226,7 +243,7 @@
         mine = pl.ds(pl.multiple_of(y * quarter, 8), quarter)
         sum_y[q][...] = part[q][mine, :] + from_y[q][0] + from_y[q][1] + from_y[q][2]
         copies = []
-        for j in range(1, NZ):
+        for j in FAR_Z:
             rows, lanes = piece(ROWS[q], (z + j) % NZ)
             copies.append(remote(sum_y[q].at[rows, lanes], from_z[q].at[j - 1], z_at(j)))
         start(copies)
@@ -240,17 +257,18 @@
             total = total + from_z[q][j]
         gather_z[q][rows, lanes] = total
         here = gather_z[q].at[rows, lanes]
-        copies = [remote(here, here, z_at(j)) for j in range(1, NZ)]
+        copies = [remote(here, here, z_at(j)) for j in FAR_Z]
         start(copies)
         return copies
 
     def spread_y(q, copies):
         quarter = ROWS[q] // 4
         arrive(copies)
-        if q == 0:
-            first = y * quarter
+        blocks, first_row, count, _ = PARTS[q]
+        if len(blocks) == 1:
+            first = blocks[0] * CM + first_row + y * quarter
         else:
-            first = CM + (y // 2) * CM + STARTS[q - 1] + (y % 2) * quarter
+            first = (blocks[0] + y // 2) * CM + first_row + (y % 2) * quarter
         rows = pl.ds(pl.multiple_of(first, 8), quarter)
         strip[rows, :] = gather_z[q][...]
         copies = [remote(gather_z[q], strip.at[rows], y_at(j)) for j in range(1, NY)]
@@ -259,59 +277,60 @@
 
     def finish(q, copies):
         arrive(copies)
-        if q == 0:
-            blocks = [(0, CM)]
-        else:
-            blocks = [(CM + STARTS[q - 1], CHUNKS[q - 1]), (2 * CM + STARTS[q - 1], CHUNKS[q - 1])]
-        for first, count in blocks:
-            at = pl.ds(first, count)
+        blocks, first_row, count, _ = PARTS[q]
+        for block in blocks:
+            at = pl.ds(block * CM + first_row, count)
             for i, term in enumerate(split_in_three(strip[at, :])):
                 terms[i, at, :] = term
 
     half = pl.multiple_of((c // 2) * HALF, HALF)
 
+    here_now = [0]
+
     def gram_part(q):
-        i = q - 1
-        first, count = STARTS[i], CHUNKS[i]
-        at_rows = pl.ds(first, count)
-        arrive([near_copies[i]])
-        part[q][...] = jnp.zeros((2 * count, 512), jnp.float32)
-
-        @pl.loop(0, NS // KT)
-        def _(s):
-            at = pl.ds(pl.multiple_of(s * KT, KT), KT)
-            part[q][:count] += lax.dot_general(
-                whiten(near[at_rows, at], at), white[:, at], NT, preferred_element_type=jnp.float32
-            )
-
-        @pl.loop(0, HALF // KT)
-        def _(s):
-            here = pl.ds(pl.multiple_of(s * KT, KT), KT)
-            at = pl.ds(pl.multiple_of(half + s * KT, KT), KT)
-            part[q][count:] += lax.dot_general(
-                whiten(near[at_rows, at], at), white_prev[:, here], NT, preferred_element_type=jnp.float32
-            )
-
-        state[q] = reduce_y(q)
-
-    state = {0: reduce_y(0)}
-
-    shadow = lax.dot_general(
-        stacked(innovation, 16), white[own, :], NT, preferred_element_type=jnp.float32
-    )
-    diagonal = jnp.sum(
-        jnp.where(eye, part[0][:, pl.ds(pl.multiple_of(k * CM, CM), CM)], 0.0), axis=0, keepdims=True
-    )
-    small[...] = jnp.concatenate(
-        [jnp.sum(shadow[:8], axis=0, keepdims=True), diagonal, jnp.zeros((6, CM), jnp.float32)], axis=0
-    )
-    small_copies = [remote(small, small_y.at[j - 1], y_at(j)) for j in range(1, NY)]
-    start(small_copies)
+        blocks, first, count, needed = PARTS[q]
+        while here_now[0] < needed:
+            arrive([near_copies[here_now[0]]])
+            here_now[0] += 1
+        part[q][...] = jnp.zeros((ROWS[q], 512), jnp.float32)
+        for place, block in enumerate(blocks):
+            to = pl.ds(place * count, count)
+            if block == 0:
+                rows = pl.ds(pl.multiple_of(k * CM + first, 128), count)
+            else:
+                rows = pl.ds(first, count)
+
+            @pl.loop(0, (HALF if block == 2 else NS) // KT)
+            def _(s):
+                here = pl.ds(pl.multiple_of(s * KT, KT), KT)
+                if block == 0:
+                    left, right = white[rows, here], white[:, here]
+                elif block == 1:
+                    left, right = whiten(near[rows, here], here), white[:, here]
+                else:
+                    at = pl.ds(pl.multiple_of(half + s * KT, KT), KT)
+                    left, right = whiten(near[rows, at], at), white_prev[:, here]
+                part[q][to] += lax.dot_general(left, right, NT, preferred_element_type=jnp.float32)
+
+    def small_sums(_):
+        shadow = lax.dot_general(
+            stacked(innovation, 16), white[own, :], NT, preferred_element_type=jnp.float32
+        )
+        mine = pl.ds(pl.multiple_of(k * CM, CM), CM)
+        square = jnp.concatenate([part[0][:, mine], part[1][:, mine]], axis=0)
+        diagonal = jnp.sum(jnp.where(eye, square, 0.0), axis=0, keepdims=True)
+        small[...] = jnp.concatenate(
+            [jnp.sum(shadow[:8], axis=0, keepdims=True), diagonal, jnp.zeros((6, CM), jnp.float32)],
+            axis=0,
+        )
+        copies = [remote(small, small_y.at[j - 1], y_at(j)) for j in range(1, NY)]
+        start(copies)
+        return copies
 
     def small_sum_y(copies):
         arrive(copies)
         small_z[NZ - 1] = small[...] + small_y[0] + small_y[1] + small_y[2]
-        copies = [remote(small_z.at[NZ - 1], small_z.at[j - 1], z_at(j)) for j in range(1, NZ)]
+        copies = [remote(small_z.at[NZ - 1], small_z.at[j - 1], z_at(j)) for j in FAR_Z]
         start(copies)
         return copies
 
@@ -321,7 +340,7 @@
         for j in range(1, NZ):
             total = total + small_z[j]
         small_m[mem] = total
-        copies = [remote(small_m.at[mem], small_m.at[mem], mem_at(j)) for j in range(1, NM)]
+        copies = [remote(small_m.at[mem], small_m.at[mem], mem_peer(j)) for j in range(1, NM)]
         start(copies)
         return copies
 
@@ -348,50 +367,40 @@
                 axis=0,
             )
 
-    def advance(stage, q):
-        state[q] = stage(q, state[q])
-
     def share_prev(i):
         arrive([prev_copies[i]])
         start([shared_copies[i]])
 
-    share_prev(0)
-    small_state = small_sum_y(small_copies)
-    advance(reduce_z, 0)
-    small_state = small_sum_z(small_state)
-    share_prev(1)
-    arrive(shared_copies)
-
-    @pl.loop(0, HALF // KT)
-    def _(s):
-        here = pl.ds(pl.multiple_of(s * KT, KT), KT)
-        at = pl.ds(pl.multiple_of(half + s * KT, KT), KT)
-        white_prev[:, here] = whiten(prev[:, here], at)
-
-    gram_part(1)
-    advance(spread_z, 0)
-    gram_part(2)
-    advance(reduce_z, 1)
-    advance(spread_y, 0)
-    gram_part(3)
-    advance(spread_z, 1)
-    advance(reduce_z, 2)
-    gram_part(4)
-    advance(reduce_z, 3)
-    advance(spread_y, 1)
-    advance(spread_z, 2)
-    advance(finish, 0)
-    advance(reduce_z, 4)
-    advance(spread_z, 3)
-    advance(spread_y, 2)
-    advance(spread_z, 4)
-    advance(spread_y, 3)
-    first_vectors(small_state)
-    advance(finish, 1)
-    advance(spread_y, 4)
-    advance(finish, 2)
-    advance(finish, 3)
-    advance(finish, 4)
+    def whiten_prev():
+        arrive(shared_copies)
+
+        @pl.loop(0, HALF // KT)
+        def _(s):
+            here = pl.ds(pl.multiple_of(s * KT, KT), KT)
+            at = pl.ds(pl.multiple_of(half + s * KT, KT), KT)
+            white_prev[:, here] = whiten(prev[:, here], at)
+
+    stages = (reduce_y, reduce_z, spread_z, spread_y, finish)
+    state = [None] * n
+    small_state = None
+    for item in ORDER:
+        if item == "prev 0":
+            share_prev(0)
+        elif item == "prev 1":
+            share_prev(1)
+        elif item == "white prev":
+            whiten_prev()
+        elif item == "small":
+            small_state = small_sums(None)
+        elif item == "small y":
+            small_state = small_sum_y(small_state)
+        elif item == "small z":
+            small_state = small_sum_z(small_state)
+        elif item == "vectors":
+            first_vectors(small_state)
+        else:
+            q, stage = item
+            state[q] = stages[stage](q, state[q])
 
     trace = small_m[0, 1:2, :]
     for j in range(1, NM):
@@ -428,7 +437,7 @@
         exchange[step, mem, :, CM : 3 * CM] = folded(for_own)
         exchange[step, mem, :, 3 * CM :] = folded(for_last)
         here = exchange.at[step, mem]
-        copies = [remote(here, here, mem_at(j)) for j in range(1, NM)]
+        copies = [remote(here, here, mem_peer(j)) for j in range(1, NM)]
         start(copies)
         arrive(copies)
         result = []
@@ -471,7 +480,7 @@
     arrive(copies)
     out_ref[group, :] = jnp.concatenate([rows_out[j, :2, :] for j in range(NY)], axis=0)
     here = out_ref.at[group]
-    copies = [remote(here, here, z_at(j)) for j in range(1, NZ)]
+    copies = [remote(here, here, z_at(j)) for j in FAR_Z]
     start(copies)
     arrive(copies)
     drain()
@@ -521,7 +530,7 @@
         out_specs=pl.BlockSpec(memory_space=pltpu.VMEM),
         scratch_shapes=scratch,
         compiler_params=pltpu.CompilerParams(
-            collective_id=0, has_side_effects=True, vmem_limit_bytes=40 * 1024 * 1024
+            collective_id=0, has_side_effects=True, vmem_limit_bytes=60 * 1024 * 1024
         ),
     )(
         class_variance,

time: 110 us -> 102 us (0.927)
  Pallas kernels: 105 us -> 100 us
  local copies, waits for them, and re-layouts: 4.95 us -> 1.47 us
    pallas_call x1, Pallas kernels: 105 us -> 100 us  [shards(): pl.pallas_call(kernel, out_shape=jax.ShapeDtypeStruct((64, CM), f32), in_...]
    unnamed x11 -> x1, local copies, waits for them, and re-layouts: 4.95 us -> 1.47 us
where the time goes in v3:
time: 102 us
  Pallas kernels  100 us (98%)
  local copies, waits for them, and re-layouts  1.47 us (1%)
    pallas_call x1, Pallas kernels, shards(): pl.pallas_call(kernel, out_shape=jax.ShapeDtypeStruct((64, CM), f32), in_...  100 us

profile of v3, /device:TPU:1, one launch (start us, length us, event | category | flops | bytes accessed | tf_op | source)
XLA Modules:
  0.0 101.7 jit_solution(13967585037124740864)
XLA Ops:
  0.0 100.2 %shard_map.55 = f32[64,256]{1,0:T(8,128)} custom-call(f32[8]{0:T(128)} %var_hbm.1, bf16[3072,256]{1,0:T(8,128)(2,1)} %m_hbm.1, f32[1,3072]{1,0:T(1,128)} %bitcast.2, s32[1,3072]{1,0:T(1,128)} %bitcast.3, f32[64,256]{1,0:T(8,128)} %ens_hbm.1), custom_call_target="tpu_custom_call" | custom-call | tf_op jit(solution)/shard_map/pallas_call | solution.py:526
  100.2 1.5 %copy.7 = f32[64,256]{1,0:T(8,128)} copy(f32[64,256]{1,0:T(8,128)} %shard_map.55) | data formatting | bytes 131072

commit v4 on v3

--- a/solution.py
+++ b/solution.py
@@ -36,7 +36,7 @@
 PREV = 2
 VR = 4
 WIDE = 5 * CM
-N_SEMS = 7 + 7 + 1 + len(CHUNKS) + 2 * PREV + 17 + 20 * len(ROWS) + 28 + 10
+N_SEMS = 4 * len(ROWS) + len(CHUNKS) + 2 * PREV + 15
 N_LOADS = NS // KT + 4
 FAR_Z = (4, 3, 5, 2, 6, 1, 7)
 NT = (((1,), (1,)), ((), ()))
@@ -90,9 +90,12 @@
 
     others = [(2, 0), (2, 1), (1, 0), (-1, 0), (1, 1), (-1, 1), (0, 1)]
 
+    def x_pair(chips, core):
+        return (dp, ((c + chips + NX) % NX) * 2 + core)
+
     def mem_peer(j):
         chips, cores = others[j - 1]
-        return (dp, ((c + chips + NX) % NX) * 2 + (k + cores) % 2)
+        return x_pair(chips, (k + cores) % 2)
 
     def y_at(offset):
         return (z * NY + (y + offset) % NY, mem)
@@ -101,33 +104,28 @@
         return (((z + offset) % NZ) * NY + y, mem)
 
     sibling = (dp, mem + 1 - 2 * k)
-    used = [0]
-    pending = []
-
-    def remote(src, dst, device):
-        i = used[0]
-        used[0] += 1
-        return pltpu.make_async_remote_copy(
-            src_ref=src,
-            dst_ref=dst,
-            send_sem=sems.at[0, i],
-            recv_sem=sems.at[1, i],
-            device_id=device,
-            device_id_type=MESH,
-        )
-
-    def start(copies):
-        for copy in copies:
-            copy.start()
-            pending.append(copy)
-
-    def arrive(copies):
-        for copy in copies:
-            copy.wait_recv()
+    started = []
+
+    def start(group, landing):
+        i = len(started)
+        for src, dst, device in group:
+            pltpu.make_async_remote_copy(
+                src_ref=src,
+                dst_ref=dst,
+                send_sem=sems.at[0, i],
+                recv_sem=sems.at[1, i],
+                device_id=device,
+                device_id_type=MESH,
+            ).start()
+        started.append(landing)
+        return i
+
+    def arrive(i):
+        pltpu.make_async_copy(started[i], started[i], sems.at[1, i]).wait()
 
     def drain():
-        while pending:
-            pending.pop(0).wait_send()
+        for i, landing in enumerate(started):
+            pltpu.make_async_copy(landing, landing, sems.at[0, i]).wait()
 
     group = pl.ds(pl.multiple_of(z * 8, 8), 8)
     fetches = []
@@ -172,31 +170,26 @@
 
     own = pl.ds(pl.multiple_of(k * CM, CM), CM)
     other = pl.ds(pl.multiple_of((1 - k) * CM, CM), CM)
-    sum_copies = [remote(sums.at[mem], sums.at[mem], mem_peer(j)) for j in range(1, NM)]
-    start(sum_copies)
-    ens_copies = [
-        remote(ensemble_in.at[mem], ensemble_in.at[mem], mem_peer(j)) for j in range(1, NM)
-    ]
-    start(ens_copies)
-    sib_copy = remote(raw, sib, sibling)
-    start([sib_copy])
+    first_seven = pl.ds(0, NM - 1)
+
+    def to_mem(here, landing):
+        return start([(here, here, mem_peer(j)) for j in range(1, NM)], landing)
+
+    sum_copies = to_mem(sums.at[mem], sums.at[first_seven])
+    ens_copies = to_mem(ensemble_in.at[mem], ensemble_in.at[first_seven])
+    sib_copy = start([(raw, sib, sibling)], raw)
     near_copies = []
     for first, count in zip(STARTS, CHUNKS, strict=True):
         at = pl.ds(first, count)
-        near_copies.append(remote(raw.at[at], near.at[at], x_at(-1)))
+        near_copies.append(start([(raw.at[at], near.at[at], x_at(-1))], raw.at[at]))
     next_half = pl.multiple_of((((c + 1) % NX) // 2) * HALF, HALF)
+    prev_rows = [
+        pl.ds(pl.multiple_of(k * CM + i * (CM // PREV), CM // PREV), CM // PREV) for i in range(PREV)
+    ]
     prev_copies, shared_copies = [], []
-    for i in range(PREV):
-        rows = CM // PREV
-        to_rows = pl.ds(pl.multiple_of(k * CM + i * rows, rows), rows)
-        prev_copies.append(
-            remote(
-                raw.at[pl.ds(i * rows, rows), pl.ds(next_half, HALF)], prev.at[to_rows], x_at(1)
-            )
-        )
-        shared_copies.append(remote(prev.at[to_rows], prev.at[to_rows], sibling))
-    start(near_copies)
-    start(prev_copies)
+    for i, to_rows in enumerate(prev_rows):
+        src = raw.at[pl.ds(i * (CM // PREV), CM // PREV), pl.ds(next_half, HALF)]
+        prev_copies.append(start([(src, prev.at[to_rows], x_at(1))], prev.at[to_rows]))
 
     classes = cls_ref[...]
     variance = jnp.zeros((1, NS), jnp.float32)
@@ -219,7 +212,7 @@
     for i in range(NS // KT):
         at = pl.ds(i * KT, KT)
         white[own, at] = whiten(raw[:, at], at)
-    arrive([sib_copy])
+    arrive(sib_copy)
 
     @pl.loop(0, NS // KT)
     def _(i):
@@ -229,25 +222,23 @@
     def reduce_y(q, _):
         gram_part(q)
         quarter = ROWS[q] // 4
-        copies = []
+        group = []
         for j in range(1, NY):
             target = (y + j) % NY
             rows = pl.ds(pl.multiple_of(target * quarter, 8), quarter)
-            copies.append(remote(part[q].at[rows], from_y[q].at[j - 1], y_at(j)))
-        start(copies)
-        return copies
+            group.append((part[q].at[rows], from_y[q].at[j - 1], y_at(j)))
+        return start(group, from_y[q])
 
     def reduce_z(q, copies):
         quarter = ROWS[q] // 4
         arrive(copies)
         mine = pl.ds(pl.multiple_of(y * quarter, 8), quarter)
         sum_y[q][...] = part[q][mine, :] + from_y[q][0] + from_y[q][1] + from_y[q][2]
-        copies = []
+        group = []
         for j in FAR_Z:
             rows, lanes = piece(ROWS[q], (z + j) % NZ)
-            copies.append(remote(sum_y[q].at[rows, lanes], from_z[q].at[j - 1], z_at(j)))
-        start(copies)
-        return copies
+            group.append((sum_y[q].at[rows, lanes], from_z[q].at[j - 1], z_at(j)))
+        return start(group, from_z[q])
 
     def spread_z(q, copies):
         arrive(copies)
@@ -257,9 +248,7 @@
             total = total + from_z[q][j]
         gather_z[q][rows, lanes] = total
         here = gather_z[q].at[rows, lanes]
-        copies = [remote(here, here, z_at(j)) for j in FAR_Z]
-        start(copies)
-        return copies
+        return start([(here, here, z_at(j)) for j in FAR_Z], from_z[q])
 
     def spread_y(q, copies):
         quarter = ROWS[q] // 4
@@ -271,9 +260,7 @@
             first = (blocks[0] + y // 2) * CM + first_row + (y % 2) * quarter
         rows = pl.ds(pl.multiple_of(first, 8), quarter)
         strip[rows, :] = gather_z[q][...]
-        copies = [remote(gather_z[q], strip.at[rows], y_at(j)) for j in range(1, NY)]
-        start(copies)
-        return copies
+        return start([(gather_z[q], strip.at[rows], y_at(j)) for j in range(1, NY)], from_y[q])
 
     def finish(q, copies):
         arrive(copies)
@@ -290,7 +277,7 @@
     def gram_part(q):
         blocks, first, count, needed = PARTS[q]
         while here_now[0] < needed:
-            arrive([near_copies[here_now[0]]])
+            arrive(near_copies[here_now[0]])
             here_now[0] += 1
         part[q][...] = jnp.zeros((ROWS[q], 512), jnp.float32)
         for place, block in enumerate(blocks):
@@ -323,16 +310,14 @@
             [jnp.sum(shadow[:8], axis=0, keepdims=True), diagonal, jnp.zeros((6, CM), jnp.float32)],
             axis=0,
         )
-        copies = [remote(small, small_y.at[j - 1], y_at(j)) for j in range(1, NY)]
-        start(copies)
-        return copies
+        return start([(small, small_y.at[j - 1], y_at(j)) for j in range(1, NY)], small_y)
 
     def small_sum_y(copies):
         arrive(copies)
         small_z[NZ - 1] = small[...] + small_y[0] + small_y[1] + small_y[2]
-        copies = [remote(small_z.at[NZ - 1], small_z.at[j - 1], z_at(j)) for j in FAR_Z]
-        start(copies)
-        return copies
+        return start(
+            [(small_z.at[NZ - 1], small_z.at[j - 1], z_at(j)) for j in FAR_Z], small_z.at[first_seven]
+        )
 
     def small_sum_z(copies):
         arrive(copies)
@@ -340,9 +325,7 @@
         for j in range(1, NZ):
             total = total + small_z[j]
         small_m[mem] = total
-        copies = [remote(small_m.at[mem], small_m.at[mem], mem_peer(j)) for j in range(1, NM)]
-        start(copies)
-        return copies
+        return to_mem(small_m.at[mem], small_m.at[first_seven])
 
     def first_vectors(copies):
         arrive(ens_copies)
@@ -368,11 +351,13 @@
             )
 
     def share_prev(i):
-        arrive([prev_copies[i]])
-        start([shared_copies[i]])
+        arrive(prev_copies[i])
+        rows = prev.at[prev_rows[i]]
+        shared_copies.append(start([(rows, rows, sibling)], rows))
 
     def whiten_prev():
-        arrive(shared_copies)
+        for copies in shared_copies:
+            arrive(copies)
 
         @pl.loop(0, HALF // KT)
         def _(s):
@@ -435,54 +420,75 @@
             )
         exchange[step, mem, :, :CM] = folded(for_next)
         exchange[step, mem, :, CM : 3 * CM] = folded(for_own)
+        mine = pl.ds(pl.multiple_of((k + 1) * CM, CM), CM)
+        exchange[step, mem, :, mine] += vec[mem]
         exchange[step, mem, :, 3 * CM :] = folded(for_last)
-        here = exchange.at[step, mem]
-        copies = [remote(here, here, mem_peer(j)) for j in range(1, NM)]
-        start(copies)
-        arrive(copies)
-        result = []
-        for chip in range(NX):
-            for core in range(2):
-                mine = slice((core + 1) * CM, (core + 2) * CM)
-                last = slice((core + 3) * CM, (core + 4) * CM)
-                above = 2 * ((chip + 1) % NX)
-                product = (
-                    exchange[step, 2 * ((chip - 1) % NX) + core, :, :CM]
-                    + exchange[step, 2 * chip, :, mine]
-                    + exchange[step, 2 * chip + 1, :, mine]
-                    + exchange[step, above, :, last]
-                    + exchange[step, above + 1, :, last]
-                )
-                result.append((product + vec[2 * chip + core]) / norm)
-        return result
-
-    moved = times(0)
-    for j in range(NM):
-        vec[j] = 1.5 * vec[j] - 0.5 * moved[j]
-        polys[j] = vec[j]
-    moved = times(1)
-    for j in range(NM):
-        vec[j] = 1.5 * vec[j] - 0.5 * moved[j]
-    moved = times(2)
-    for j in range(NM):
-        vec[j] = moved[j]
-    moved = times(3)
+        def block(lanes):
+            return exchange.at[step, mem, :, lanes]
+
+        def landing(count, lanes):
+            return exchange.at[step, pl.ds(0, count), :, pl.ds(0, lanes)]
+
+        if step == 1:
+            across_ring = [x_pair(2, core) for core in range(2)]
+            far = [(block(pl.ds(0, CM)),) * 2 + (device,) for device in across_ring]
+            for core, device in enumerate(across_ring):
+                lanes = pl.ds((3 + core) * CM, CM)
+                far.append((block(lanes), block(lanes), device))
+            ahead_part, rest = block(pl.ds(0, 3 * CM)), block(pl.ds(CM, 4 * CM))
+            groups = [
+                start(far, landing(4, CM)),
+                start([(ahead_part, ahead_part, x_pair(1, core)) for core in range(2)], landing(2, 3 * CM)),
+                start([(rest, rest, x_pair(-1, core)) for core in range(2)], landing(2, 4 * CM)),
+                start([(rest, rest, sibling)], landing(1, 4 * CM)),
+            ]
+        else:
+            groups = [to_mem(exchange.at[step, mem], exchange.at[step, first_seven])]
+        for copies in groups:
+            arrive(copies)
+
+    def product(step, chip, core):
+        mine = pl.ds(pl.multiple_of((core + 1) * CM, CM), CM)
+        last = pl.ds(pl.multiple_of((core + 3) * CM, CM), CM)
+        below, above = 2 * ((chip + NX - 1) % NX), 2 * ((chip + 1) % NX)
+        at = 2 * chip
+        whole = (
+            exchange[step, below + core, :, pl.ds(0, CM)]
+            + exchange[step, at, :, mine]
+            + exchange[step, at + 1, :, mine]
+            + exchange[step, above, :, last]
+            + exchange[step, above + 1, :, last]
+        )
+        return whole / norm
+
+    everyone = [(chip, core) for chip in range(NX) for core in range(2)]
+    neighbours = [(c, 0), (c, 1), ((c + 1) % NX, k), ((c + NX - 1) % NX, 0), ((c + NX - 1) % NX, 1)]
+
+    def apply(step, pieces, update):
+        times(step)
+        moved = [product(step, chip, core) for chip, core in pieces]
+        for (chip, core), value in zip(pieces, moved, strict=True):
+            at = 2 * chip + core
+            vec[at] = update(vec[at], value)
+
+    apply(0, everyone, lambda old, value: 1.5 * old - 0.5 * value)
+    polys[...] = vec[...]
+    apply(1, neighbours, lambda old, value: 1.5 * old - 0.5 * value)
+    apply(2, everyone, lambda old, value: value)
+    times(3)
     shift = jnp.zeros((2, 1), jnp.float32)
-    for j in range(NM):
-        applied = 1.5 * polys[j] - 0.5 * (1.5 * vec[j] - 0.5 * moved[j])
-        polys[j] = applied
+    for chip, core in everyone:
+        at = 2 * chip + core
+        applied = 1.5 * polys[at] - 0.5 * (1.5 * vec[at] - 0.5 * product(3, chip, core))
+        polys[at] = applied
         shift = shift + jnp.sum(applied[:2] * applied[2:3], axis=1, keepdims=True)
     shift = shift / norm / math.sqrt(MEMBERS - 1)
     rows_out[y, :2, :] = centers[:2, :1] + shift + polys[mem][:2] / jnp.sqrt(norm)
     here = rows_out.at[y]
-    copies = [remote(here, here, y_at(j)) for j in range(1, NY)]
-    start(copies)
-    arrive(copies)
+    arrive(start([(here, here, y_at(j)) for j in range(1, NY)], rows_out.at[pl.ds(0, NY - 1)]))
     out_ref[group, :] = jnp.concatenate([rows_out[j, :2, :] for j in range(NY)], axis=0)
     here = out_ref.at[group]
-    copies = [remote(here, here, z_at(j)) for j in FAR_Z]
-    start(copies)
-    arrive(copies)
+    arrive(start([(here, here, z_at(j)) for j in FAR_Z], out_ref.at[pl.ds(0, 8 * (NZ - 1))]))
     drain()
 
 

time: 102 us -> 97.6 us (0.957)
  Pallas kernels: 100 us -> 96 us
    pallas_call x1, Pallas kernels: 100 us -> 96 us  [shards(): pl.pallas_call(kernel, out_shape=jax.ShapeDtypeStruct((64, CM), f32), in_...]
where the time goes in v4:
time: 97.6 us; the launch traced here: 97.5 us
  Pallas kernels  96 us (98%)
  local copies, waits for them, and re-layouts  1.47 us (2%)
    pallas_call x1, Pallas kernels, shards(): pl.pallas_call(kernel, out_shape=jax.ShapeDtypeStruct((64, CM), f32), in_...  96 us

profile of v4, /device:TPU:1, one launch (start us, length us, event | category | flops | bytes accessed | tf_op | source)
XLA Modules:
  0.0 97.5 jit_solution(2779642680892814020)
XLA Ops:
  0.0 96.0 %shard_map.55 = f32[64,256]{1,0:T(8,128)} custom-call(f32[8]{0:T(128)} %var_hbm.1, bf16[3072,256]{1,0:T(8,128)(2,1)} %m_hbm.1, f32[1,3072]{1,0:T(1,128)} %bitcast.2, s32[1,3072]{1,0:T(1,128)} %bitcast.3, f32[64,256]{1,0:T(8,128)} %ens_hbm.1), custom_call_target="tpu_custom_call" | custom-call | tf_op jit(solution)/shard_map/pallas_call | solution.py:532
  96.0 1.5 %copy.7 = f32[64,256]{1,0:T(8,128)} copy(f32[64,256]{1,0:T(8,128)} %shard_map.55) | data formatting | bytes 131072

commit v5 on v4

--- a/solution.py
+++ b/solution.py
@@ -36,7 +36,7 @@
 PREV = 2
 VR = 4
 WIDE = 5 * CM
-N_SEMS = 4 * len(ROWS) + len(CHUNKS) + 2 * PREV + 15
+N_SEMS = 4 * len(ROWS) + len(CHUNKS) + 1 + PREV + 1 + 3 + 3 + 7 + 2
 N_LOADS = NS // KT + 4
 FAR_Z = (4, 3, 5, 2, 6, 1, 7)
 NT = (((1,), (1,)), ((), ()))
@@ -75,9 +75,9 @@
     (
         m_ref, obs_ref, cls_ref, var_ref, raw, near, prev, sib, white, white_prev, sums, scale, bases,
         ensemble_in, centers, small, small_y, small_z, small_m, strip, terms, vec, polys, exchange,
-        rows_out, loads, sems,
-    ) = scratch[:27]
-    lists = scratch[27:]
+        rows_out, norms, tally, loads, sems,
+    ) = scratch[:29]
+    lists = scratch[29:]
     n = len(ROWS)
     part, from_y, sum_y, from_z, gather_z = (lists[i * n : (i + 1) * n] for i in range(5))
 
@@ -106,8 +106,10 @@
     sibling = (dp, mem + 1 - 2 * k)
     started = []
 
-    def start(group, landing):
-        i = len(started)
+    def start(group, landing, i=None):
+        if i is None:
+            i = len(started)
+            started.append(landing)
         for src, dst, device in group:
             pltpu.make_async_remote_copy(
                 src_ref=src,
@@ -117,7 +119,6 @@
                 device_id=device,
                 device_id_type=MESH,
             ).start()
-        started.append(landing)
         return i
 
     def arrive(i):
@@ -176,20 +177,29 @@
         return start([(here, here, mem_peer(j)) for j in range(1, NM)], landing)
 
     sum_copies = to_mem(sums.at[mem], sums.at[first_seven])
-    ens_copies = to_mem(ensemble_in.at[mem], ensemble_in.at[first_seven])
-    sib_copy = start([(raw, sib, sibling)], raw)
     near_copies = []
     for first, count in zip(STARTS, CHUNKS, strict=True):
-        at = pl.ds(first, count)
-        near_copies.append(start([(raw.at[at], near.at[at], x_at(-1))], raw.at[at]))
+        rows = pl.ds(first, count)
+        if first + count < CM:
+            near_copies.append([start([(raw.at[rows], near.at[rows], x_at(-1))], raw.at[rows])])
+            continue
+        halves = []
+        for turn_of in range(2):
+            lanes = pl.ds(pl.multiple_of((((c + 3) % NX) // 2 + turn_of) % 2 * HALF, HALF), HALF)
+            src, dst = raw.at[rows, lanes], near.at[rows, lanes]
+            halves.append(start([(src, dst, x_at(-1))], dst))
+        near_copies.append(halves)
     next_half = pl.multiple_of((((c + 1) % NX) // 2) * HALF, HALF)
     prev_rows = [
         pl.ds(pl.multiple_of(k * CM + i * (CM // PREV), CM // PREV), CM // PREV) for i in range(PREV)
     ]
-    prev_copies, shared_copies = [], []
+    prev_copies = []
     for i, to_rows in enumerate(prev_rows):
         src = raw.at[pl.ds(i * (CM // PREV), CM // PREV), pl.ds(next_half, HALF)]
         prev_copies.append(start([(src, prev.at[to_rows], x_at(1))], prev.at[to_rows]))
+    shared_copies = []
+    sib_copy = start([(raw, sib, sibling)], raw)
+    ens_copies = to_mem(ensemble_in.at[mem], ensemble_in.at[first_seven])
 
     classes = cls_ref[...]
     variance = jnp.zeros((1, NS), jnp.float32)
@@ -272,32 +282,34 @@
 
     half = pl.multiple_of((c // 2) * HALF, HALF)
 
+    other_half = pl.multiple_of((1 - c // 2) * HALF, HALF)
     here_now = [0]
+
+    def times_gram(left, right):
+        return lax.dot_general(left, right, NT, preferred_element_type=jnp.float32)
 
     def gram_part(q):
         blocks, first, count, needed = PARTS[q]
         while here_now[0] < needed:
-            arrive(near_copies[here_now[0]])
+            arrive(near_copies[here_now[0]][0])
             here_now[0] += 1
-        part[q][...] = jnp.zeros((ROWS[q], 512), jnp.float32)
-        for place, block in enumerate(blocks):
-            to = pl.ds(place * count, count)
-            if block == 0:
-                rows = pl.ds(pl.multiple_of(k * CM + first, 128), count)
-            else:
-                rows = pl.ds(first, count)
-
-            @pl.loop(0, (HALF if block == 2 else NS) // KT)
-            def _(s):
-                here = pl.ds(pl.multiple_of(s * KT, KT), KT)
-                if block == 0:
-                    left, right = white[rows, here], white[:, here]
-                elif block == 1:
-                    left, right = whiten(near[rows, here], here), white[:, here]
-                else:
-                    at = pl.ds(pl.multiple_of(half + s * KT, KT), KT)
-                    left, right = whiten(near[rows, at], at), white_prev[:, here]
-                part[q][to] += lax.dot_general(left, right, NT, preferred_element_type=jnp.float32)
+        if blocks == (0,):
+            rows = pl.ds(pl.multiple_of(k * CM + first, 128), count)
+            part[q][...] = sum(
+                times_gram(white[rows, at], white[:, at]) for at in (pl.ds(0, HALF), pl.ds(HALF, HALF))
+            )
+            return
+        rows = pl.ds(first, count)
+        at = pl.ds(half, HALF)
+        left = whiten(near[rows, at], at)
+        if 2 in blocks:
+            part[q][pl.ds((len(blocks) - 1) * count, count)] = times_gram(left, white_prev[...])
+        if 1 in blocks:
+            total = times_gram(left, white[:, at])
+            for copies in near_copies[needed - 1][1:]:
+                arrive(copies)
+            at = pl.ds(other_half, HALF)
+            part[q][:count] = total + times_gram(whiten(near[rows, at], at), white[:, at])
 
     def small_sums(_):
         shadow = lax.dot_general(
@@ -335,6 +347,11 @@
             center = center + ensemble_in[j].sum(axis=1, keepdims=True)
         center = center / MEMBERS
         place = lax.broadcasted_iota(jnp.int32, (8, 1), 0)
+        trace = small_m[0, 1:2, :]
+        for j in range(1, NM):
+            trace = trace + small_m[j, 1:2, :]
+        norm = (MEMBERS + jnp.sum(trace, axis=1, keepdims=True)) / MEMBERS
+        norms[...] = jnp.broadcast_to(norm, (8, 128))
 
         def own_rows(block):
             return [
@@ -353,11 +370,13 @@
     def share_prev(i):
         arrive(prev_copies[i])
         rows = prev.at[prev_rows[i]]
-        shared_copies.append(start([(rows, rows, sibling)], rows))
+        if i == 0:
+            shared_copies.append(start([(rows, rows, sibling)], prev.at[pl.ds(0, CM)]))
+        else:
+            start([(rows, rows, sibling)], None, shared_copies[0])
 
     def whiten_prev():
-        for copies in shared_copies:
-            arrive(copies)
+        arrive(shared_copies[0])
 
         @pl.loop(0, HALF // KT)
         def _(s):
@@ -387,65 +406,59 @@
             q, stage = item
             state[q] = stages[stage](q, state[q])
 
-    trace = small_m[0, 1:2, :]
-    for j in range(1, NM):
-        trace = trace + small_m[j, 1:2, :]
-    norm = (MEMBERS + jnp.sum(trace, axis=1, keepdims=True)) / MEMBERS
+    norm = norms[:1, :1]
 
     def folded(rows):
         return rows[:VR] + rows[VR : 2 * VR] + rows[2 * VR : 3 * VR]
 
+    behind = ((c + NX - 1) % NX) * 2
+    ring = [x_pair(2, core) for core in range(2)]
+
     def times(step):
         ahead = vec[((c + 1) % NX) * 2 + k]
-        behind = ((c + NX - 1) % NX) * 2
         down = stacked(jnp.concatenate([vec[mem], ahead], axis=1), 4 * VR)
         across = stacked(jnp.concatenate([vec[2 * c], vec[2 * c + 1]], axis=1), 4 * VR)
         back = stacked(jnp.concatenate([vec[behind], vec[behind + 1]], axis=1), 4 * VR)
         for_next = for_own = for_last = 0.0
         for i in range(3):
-            for_next = (
-                for_next
-                + lax.dot_general(
-                    across, terms[i, CM : 2 * CM, :], NT, preferred_element_type=jnp.float32
-                )
-                + lax.dot_general(
-                    back, terms[i, 2 * CM :, :], NT, preferred_element_type=jnp.float32
-                )
-            )
-            for_own = for_own + jnp.dot(
-                down, terms[i, : 2 * CM, :], preferred_element_type=jnp.float32
-            )
+            for_next = for_next + times_gram(across, terms[i, CM : 2 * CM, :])
+            for_next = for_next + times_gram(back, terms[i, 2 * CM :, :])
             for_last = for_last + jnp.dot(
                 down[:, CM:], terms[i, 2 * CM :, :], preferred_element_type=jnp.float32
             )
         exchange[step, mem, :, :CM] = folded(for_next)
+        exchange[step, mem, :, 3 * CM :] = folded(for_last)
+
+        def same(first, count, device):
+            here = exchange.at[step, mem, :, pl.ds(pl.multiple_of(first * CM, CM), count * CM)]
+            return here, here, device
+
+        def pair(first, count, chips):
+            return [same(first, count, x_pair(chips, core)) for core in range(2)]
+
+        needed = start(
+            pair(0, 1, 2) + [same(3 + core, 1, device) for core, device in enumerate(ring)],
+            tally.at[pl.ds(0, 22)],
+        )
+        for i in range(3):
+            for_own = for_own + jnp.dot(
+                down, terms[i, : 2 * CM, :], preferred_element_type=jnp.float32
+            )
         exchange[step, mem, :, CM : 3 * CM] = folded(for_own)
         mine = pl.ds(pl.multiple_of((k + 1) * CM, CM), CM)
         exchange[step, mem, :, mine] += vec[mem]
-        exchange[step, mem, :, 3 * CM :] = folded(for_last)
-        def block(lanes):
-            return exchange.at[step, mem, :, lanes]
-
-        def landing(count, lanes):
-            return exchange.at[step, pl.ds(0, count), :, pl.ds(0, lanes)]
-
+        start(pair(0, 3, 1) + pair(1, 4, -1) + [same(1, 4, sibling)], None, needed)
         if step == 1:
-            across_ring = [x_pair(2, core) for core in range(2)]
-            far = [(block(pl.ds(0, CM)),) * 2 + (device,) for device in across_ring]
-            for core, device in enumerate(across_ring):
-                lanes = pl.ds((3 + core) * CM, CM)
-                far.append((block(lanes), block(lanes), device))
-            ahead_part, rest = block(pl.ds(0, 3 * CM)), block(pl.ds(CM, 4 * CM))
-            groups = [
-                start(far, landing(4, CM)),
-                start([(ahead_part, ahead_part, x_pair(1, core)) for core in range(2)], landing(2, 3 * CM)),
-                start([(rest, rest, x_pair(-1, core)) for core in range(2)], landing(2, 4 * CM)),
-                start([(rest, rest, sibling)], landing(1, 4 * CM)),
-            ]
-        else:
-            groups = [to_mem(exchange.at[step, mem], exchange.at[step, first_seven])]
-        for copies in groups:
-            arrive(copies)
+            return needed, None
+        late = start(
+            pair(1, 2, 2)
+            + [same(4 - core, 1, device) for core, device in enumerate(ring)]
+            + pair(3, 2, 1)
+            + pair(0, 1, -1)
+            + [same(0, 1, sibling)],
+            tally.at[pl.ds(0, 13)],
+        )
+        return needed, late
 
     def product(step, chip, core):
         mine = pl.ds(pl.multiple_of((core + 1) * CM, CM), CM)
@@ -461,27 +474,44 @@
         )
         return whole / norm
 
-    everyone = [(chip, core) for chip in range(NX) for core in range(2)]
     neighbours = [(c, 0), (c, 1), ((c + 1) % NX, k), ((c + NX - 1) % NX, 0), ((c + NX - 1) % NX, 1)]
-
-    def apply(step, pieces, update):
-        times(step)
-        moved = [product(step, chip, core) for chip, core in pieces]
-        for (chip, core), value in zip(pieces, moved, strict=True):
+    distant = [((c + 1) % NX, 1 - k), ((c + 2) % NX, 0), ((c + 2) % NX, 1)]
+
+    def advanced(step, pieces, update):
+        for chip, core in pieces:
             at = 2 * chip + core
-            vec[at] = update(vec[at], value)
-
-    apply(0, everyone, lambda old, value: 1.5 * old - 0.5 * value)
-    polys[...] = vec[...]
-    apply(1, neighbours, lambda old, value: 1.5 * old - 0.5 * value)
-    apply(2, everyone, lambda old, value: value)
-    times(3)
+            vec[at] = update(vec[at], product(step, chip, core))
+
+    def one_step(old, value):
+        return 1.5 * old - 0.5 * value
+
+    needed, late = times(0)
+    arrive(needed)
+    advanced(0, neighbours, one_step)
+    for chip, core in neighbours:
+        polys[2 * chip + core] = vec[2 * chip + core]
+    needed, _ = times(1)
+    arrive(late)
+    advanced(0, distant, one_step)
+    for chip, core in distant:
+        polys[2 * chip + core] = vec[2 * chip + core]
+    arrive(needed)
+    advanced(1, neighbours, one_step)
+    needed, late = times(2)
+    arrive(needed)
+    advanced(2, neighbours, lambda old, value: value)
+    needed, last = times(3)
+    arrive(late)
+    advanced(2, distant, lambda old, value: value)
+    arrive(needed)
+    arrive(last)
     shift = jnp.zeros((2, 1), jnp.float32)
-    for chip, core in everyone:
-        at = 2 * chip + core
-        applied = 1.5 * polys[at] - 0.5 * (1.5 * vec[at] - 0.5 * product(3, chip, core))
-        polys[at] = applied
-        shift = shift + jnp.sum(applied[:2] * applied[2:3], axis=1, keepdims=True)
+    for chip in range(NX):
+        for core in range(2):
+            at = 2 * chip + core
+            applied = 1.5 * polys[at] - 0.5 * (1.5 * vec[at] - 0.5 * product(3, chip, core))
+            polys[at] = applied
+            shift = shift + jnp.sum(applied[:2] * applied[2:3], axis=1, keepdims=True)
     shift = shift / norm / math.sqrt(MEMBERS - 1)
     rows_out[y, :2, :] = centers[:2, :1] + shift + polys[mem][:2] / jnp.sqrt(norm)
     here = rows_out.at[y]
@@ -521,6 +551,8 @@
         pltpu.VMEM((NM, VR, CM), f32),
         pltpu.VMEM((4, NM, VR, WIDE), f32),
         pltpu.VMEM((NY, 8, CM), f32),
+        pltpu.VMEM((8, 128), f32),
+        pltpu.VMEM((22, VR, CM), f32),
         pltpu.SemaphoreType.DMA((N_LOADS,)),
         pltpu.SemaphoreType.DMA((2, N_SEMS)),
     ]

time: 97.6 us -> 95.7 us (0.981)
  Pallas kernels: 96 us -> 94.1 us
    pallas_call x1, Pallas kernels: 96 us -> 94.1 us  [shards(): pl.pallas_call(kernel, out_shape=jax.ShapeDtypeStruct((64, CM), f32), in_...]
where the time goes in v5:
time: 95.7 us; the launch traced here: 95.5 us
  Pallas kernels  94.1 us (98%)
  local copies, waits for them, and re-layouts  1.47 us (2%)
    pallas_call x1, Pallas kernels, shards(): pl.pallas_call(kernel, out_shape=jax.ShapeDtypeStruct((64, CM), f32), in_...  94.1 us

profile of v5, /device:TPU:1, one launch (start us, length us, event | category | flops | bytes accessed | tf_op | source)
XLA Modules:
  0.0 95.5 jit_solution(13776792126690504002)
XLA Ops:
  0.0 94.1 %shard_map.55 = f32[64,256]{1,0:T(8,128)} custom-call(f32[8]{0:T(128)} %var_hbm.1, bf16[3072,256]{1,0:T(8,128)(2,1)} %m_hbm.1, f32[1,3072]{1,0:T(1,128)} %bitcast.2, s32[1,3072]{1,0:T(1,128)} %bitcast.3, f32[64,256]{1,0:T(8,128)} %ens_hbm.1), custom_call_target="tpu_custom_call" | custom-call | tf_op jit(solution)/shard_map/pallas_call | solution.py:564
  94.1 1.5 %copy.7 = f32[64,256]{1,0:T(8,128)} copy(f32[64,256]{1,0:T(8,128)} %shard_map.55) | data formatting | bytes 131072

commit v6 on v5

--- a/solution.py
+++ b/solution.py
@@ -75,9 +75,9 @@
     (
         m_ref, obs_ref, cls_ref, var_ref, raw, near, prev, sib, white, white_prev, sums, scale, bases,
         ensemble_in, centers, small, small_y, small_z, small_m, strip, terms, vec, polys, exchange,
-        rows_out, norms, tally, loads, sems,
-    ) = scratch[:29]
-    lists = scratch[29:]
+        rows_out, plane, norms, tally, loads, sems,
+    ) = scratch[:30]
+    lists = scratch[30:]
     n = len(ROWS)
     part, from_y, sum_y, from_z, gather_z = (lists[i * n : (i + 1) * n] for i in range(5))
 
@@ -124,9 +124,21 @@
     def arrive(i):
         pltpu.make_async_copy(started[i], started[i], sems.at[1, i]).wait()
 
+    drained = [0]
+
     def drain():
-        for i, landing in enumerate(started):
-            pltpu.make_async_copy(landing, landing, sems.at[0, i]).wait()
+        for i in range(drained[0], len(started)):
+            pltpu.make_async_copy(started[i], started[i], sems.at[0, i]).wait()
+        drained[0] = len(started)
+
+    barrier = pltpu.get_barrier_semaphore()
+    greeted = (
+        [z_at(j) for j in FAR_Z]
+        + [y_at(j) for j in (2, 1, 3)]
+        + [mem_peer(j) for j in range(1, NM)]
+    )
+    for device in greeted:
+        pl.semaphore_signal(barrier, inc=1, device_id=device, device_id_type=MESH)
 
     group = pl.ds(pl.multiple_of(z * 8, 8), 8)
     fetches = []
@@ -143,30 +155,19 @@
     for fetch in fetches:
         fetch.start()
 
-    barrier = pltpu.get_barrier_semaphore()
-    greeted = (
-        [mem_peer(j) for j in range(1, NM)]
-        + [y_at(j) for j in range(1, NY)]
-        + [z_at(j) for j in range(1, NZ)]
-    )
-    for device in greeted:
-        pl.semaphore_signal(barrier, inc=1, device_id=device, device_id_type=MESH)
-
     eye = (
         lax.broadcasted_iota(jnp.int32, (CM, CM), 0) == lax.broadcasted_iota(jnp.int32, (CM, CM), 1)
     )
-    turn = jnp.concatenate(
-        [jnp.where(eye, 1.0, 0.0), jnp.ones((16, CM), jnp.float32)], axis=0
+    first_rows = jnp.concatenate(
+        [jnp.where(eye, 1.0, 0.0)[: CHUNKS[0]], jnp.ones((16, CM), jnp.float32)], axis=0
     ).astype(jnp.bfloat16)
+    other_rows = jnp.where(eye, 1.0, 0.0)[CHUNKS[0] :].astype(jnp.bfloat16)
     for i in range(NS // KT):
         at = pl.ds(i * KT, KT)
         fetches[i].wait()
-        turned = lax.dot_general(turn, m_ref[at, :], NT, preferred_element_type=jnp.float32)
-        raw[:, at] = turned[:CM].astype(jnp.bfloat16)
-        sums[mem, :, at] = turned[CM : CM + 1]
-    for fetch in fetches[NS // KT :]:
-        fetch.wait()
-
+        turned = lax.dot_general(first_rows, m_ref[at, :], NT, preferred_element_type=jnp.float32)
+        raw[: CHUNKS[0], at] = turned[: CHUNKS[0]].astype(jnp.bfloat16)
+        sums[mem, :, at] = turned[CHUNKS[0] : CHUNKS[0] + 1]
     pl.semaphore_wait(barrier, len(greeted))
 
     own = pl.ds(pl.multiple_of(k * CM, CM), CM)
@@ -180,6 +181,15 @@
     near_copies = []
     for first, count in zip(STARTS, CHUNKS, strict=True):
         rows = pl.ds(first, count)
+        if first == CHUNKS[0]:
+
+            @pl.loop(0, NS // KT)
+            def _(i):
+                at = pl.ds(pl.multiple_of(i * KT, KT), KT)
+                raw[CHUNKS[0] :, at] = lax.dot_general(
+                    other_rows, m_ref[at, :], NT, preferred_element_type=jnp.float32
+                ).astype(jnp.bfloat16)
+
         if first + count < CM:
             near_copies.append([start([(raw.at[rows], near.at[rows], x_at(-1))], raw.at[rows])])
             continue
@@ -199,6 +209,8 @@
         prev_copies.append(start([(src, prev.at[to_rows], x_at(1))], prev.at[to_rows]))
     shared_copies = []
     sib_copy = start([(raw, sib, sibling)], raw)
+    for fetch in fetches[NS // KT :]:
+        fetch.wait()
     ens_copies = to_mem(ensemble_in.at[mem], ensemble_in.at[first_seven])
 
     classes = cls_ref[...]
@@ -490,7 +502,11 @@
     advanced(0, neighbours, one_step)
     for chip, core in neighbours:
         polys[2 * chip + core] = vec[2 * chip + core]
+    before = len(started)
     needed, _ = times(1)
+    for i in range(before):
+        pltpu.make_async_copy(started[i], started[i], sems.at[0, i]).wait()
+    drained[0] = before
     arrive(late)
     advanced(0, distant, one_step)
     for chip, core in distant:
@@ -516,9 +532,13 @@
     rows_out[y, :2, :] = centers[:2, :1] + shift + polys[mem][:2] / jnp.sqrt(norm)
     here = rows_out.at[y]
     arrive(start([(here, here, y_at(j)) for j in range(1, NY)], rows_out.at[pl.ds(0, NY - 1)]))
-    out_ref[group, :] = jnp.concatenate([rows_out[j, :2, :] for j in range(NY)], axis=0)
+    plane[...] = jnp.concatenate([rows_out[j, :2, :] for j in range(NY)], axis=0)
     here = out_ref.at[group]
-    arrive(start([(here, here, z_at(j)) for j in FAR_Z], out_ref.at[pl.ds(0, 8 * (NZ - 1))]))
+    planes = start([(plane, here, z_at(j)) for j in FAR_Z], out_ref.at[pl.ds(0, 8 * (NZ - 1))])
+    stored = pltpu.make_async_copy(plane, here, loads.at[0])
+    stored.start()
+    arrive(planes)
+    stored.wait()
     drain()
 
 
@@ -551,6 +571,7 @@
         pltpu.VMEM((NM, VR, CM), f32),
         pltpu.VMEM((4, NM, VR, WIDE), f32),
         pltpu.VMEM((NY, 8, CM), f32),
+        pltpu.VMEM((8, CM), f32),
         pltpu.VMEM((8, 128), f32),
         pltpu.VMEM((22, VR, CM), f32),
         pltpu.SemaphoreType.DMA((N_LOADS,)),
@@ -565,7 +586,7 @@
         kernel,
         out_shape=jax.ShapeDtypeStruct((64, CM), f32),
         in_specs=[hbm] * 5,
-        out_specs=pl.BlockSpec(memory_space=pltpu.VMEM),
+        out_specs=hbm,
         scratch_shapes=scratch,
         compiler_params=pltpu.CompilerParams(
             collective_id=0, has_side_effects=True, vmem_limit_bytes=60 * 1024 * 1024

time: 95.7 us -> 94.9 us (level)
  no operation moved by 1% of the time
where the time goes in v6:
time: 94.9 us; the launch traced here: 94.8 us
  Pallas kernels  93.3 us (98%)
  local copies, waits for them, and re-layouts  1.47 us (2%)
    pallas_call x1, Pallas kernels, shards(): pl.pallas_call(kernel, out_shape=jax.ShapeDtypeStruct((64, CM), f32), in_...  93.3 us

profile of v6, /device:TPU:1, one launch (start us, length us, event | category | flops | bytes accessed | tf_op | source)
XLA Modules:
  0.0 94.8 jit_solution(6584003326412972186)
XLA Ops:
  0.0 93.3 %shard_map.55 = f32[64,256]{1,0:T(8,128)} custom-call(f32[8]{0:T(128)} %var_hbm.1, bf16[3072,256]{1,0:T(8,128)(2,1)} %m_hbm.1, f32[1,3072]{1,0:T(1,128)} %bitcast.2, s32[1,3072]{1,0:T(1,128)} %bitcast.3, f32[64,256]{1,0:T(8,128)} %ens_hbm.1), custom_call_target="tpu_custom_call" | custom-call | tf_op jit(solution)/shard_map/pallas_call | solution.py:585
  93.3 1.5 %copy.7 = f32[64,256]{1,0:T(8,128)} copy(f32[64,256]{1,0:T(8,128)} %shard_map.55) | data formatting | bytes 131072

commit v7 on v6

--- a/solution.py
+++ b/solution.py
@@ -14,7 +14,7 @@
 NS = 3072
 HALF = NS // 2
 KT = 512
-CHUNKS = (64, 64, 64, 32, 32)
+CHUNKS = (64, 64, 32, 32, 32, 16, 16)
 STARTS = tuple(sum(CHUNKS[:i]) for i in range(len(CHUNKS)))
 PARTS = (
     ((0,), 0, 128, 0),
@@ -22,17 +22,21 @@
     ((1,), 0, 64, 1),
     ((1,), 64, 64, 2),
     ((2,), 0, 128, 2),
-    ((1, 2), 128, 64, 3),
-    ((1, 2), 192, 32, 4),
-    ((1, 2), 224, 32, 5),
+    ((1, 2), 128, 32, 3),
+    ((1, 2), 160, 32, 4),
+    ((1, 2), 192, 32, 5),
+    ((1, 2), 224, 16, 6),
+    ((1, 2), 240, 16, 7),
 )
 ROWS = tuple(len(blocks) * count for blocks, _, count, _ in PARTS)
 ORDER = (
-    (0, 0), (1, 0), "small", (2, 0), "prev 0", (2, 1), (0, 1), (1, 1), "prev 1", (3, 0), "white prev", (4, 0),
-    (2, 2), "small y", (3, 1), (1, 2), (5, 0), (0, 2), (4, 1), (3, 2), "small z", (1, 3), (6, 0), (5, 1), (7, 0),
-    (0, 3), (4, 2), (6, 1), (2, 3), (3, 3), (7, 1), (5, 2), (4, 3), (6, 2), (7, 2), (5, 3), (1, 4), (6, 3),
-    "vectors", (7, 3), (0, 4), (4, 4), (6, 4), (5, 4), (3, 4), (2, 4), (7, 4),
+    (0, 0), (1, 0), "small", (2, 0), "small y", "prev 0", (0, 1), (1, 1), "prev 1", (3, 0), (0, 2),
+    "white prev", (4, 0), (2, 1), (3, 1), (5, 0), (1, 2), "small z", (6, 0), (4, 1), (2, 2), (0, 3),
+    (5, 1), (7, 0), (3, 2), (6, 1), (8, 0), (4, 2), (9, 0), (5, 2), (7, 1), (1, 3), (8, 1), (3, 3), (0, 4),
+    (6, 2), (9, 1), (5, 3), (4, 3), (7, 2), (8, 2), (2, 3), (6, 3), (9, 2), (7, 3), "vectors", (5, 4),
+    (3, 4), (6, 4), (1, 4), (4, 4), (8, 3), (2, 4), (9, 3), (7, 4),
 )
+SHORT = 32
 PREV = 2
 VR = 4
 WIDE = 5 * CM
@@ -53,6 +57,8 @@
 
 
 def piece_shape(rows):
+    if rows == SHORT:
+        return (rows // 4, 512)
     return (8, 512 // (NZ // (rows // 4 // 8)))
 
 
@@ -262,6 +268,20 @@
             group.append((sum_y[q].at[rows, lanes], from_z[q].at[j - 1], z_at(j)))
         return start(group, from_z[q])
 
+    def exchange_z(q, copies):
+        arrive(copies)
+        mine = pl.ds(pl.multiple_of(y * (ROWS[q] // 4), 8), ROWS[q] // 4)
+        sum_y[q][...] = part[q][mine, :] + from_y[q][0] + from_y[q][1] + from_y[q][2]
+        return start([(sum_y[q], from_z[q].at[j - 1], z_at(j)) for j in FAR_Z], from_z[q])
+
+    def spread_sum(q, copies):
+        arrive(copies)
+        total = sum_y[q][...]
+        for j in range(NZ - 1):
+            total = total + from_z[q][j]
+        gather_z[q][...] = total
+        return give_y(q)
+
     def spread_z(q, copies):
         arrive(copies)
         rows, lanes = piece(ROWS[q], z)
@@ -273,8 +293,11 @@
         return start([(here, here, z_at(j)) for j in FAR_Z], from_z[q])
 
     def spread_y(q, copies):
+        arrive(copies)
+        return give_y(q)
+
+    def give_y(q):
         quarter = ROWS[q] // 4
-        arrive(copies)
         blocks, first_row, count, _ = PARTS[q]
         if len(blocks) == 1:
             first = blocks[0] * CM + first_row + y * quarter
@@ -396,7 +419,8 @@
             at = pl.ds(pl.multiple_of(half + s * KT, KT), KT)
             white_prev[:, here] = whiten(prev[:, here], at)
 
-    stages = (reduce_y, reduce_z, spread_z, spread_y, finish)
+    usual = (reduce_y, reduce_z, spread_z, spread_y, finish)
+    short = (reduce_y, exchange_z, spread_sum, finish)
     state = [None] * n
     small_state = None
     for item in ORDER:
@@ -416,7 +440,7 @@
             first_vectors(small_state)
         else:
             q, stage = item
-            state[q] = stages[stage](q, state[q])
+            state[q] = (short if ROWS[q] == SHORT else usual)[stage](q, state[q])
 
     norm = norms[:1, :1]
 

time: 94.9 us -> 93.2 us (0.982)
  Pallas kernels: 93.3 us -> 91.6 us
    pallas_call x1, Pallas kernels: 93.3 us -> 91.6 us  [shards(): pl.pallas_call(kernel, out_shape=jax.ShapeDtypeStruct((64, CM), f32), in_...]
where the time goes in v7:
time: 93.2 us; the launch traced here: 93.1 us
  Pallas kernels  91.6 us (98%)
  local copies, waits for them, and re-layouts  1.47 us (2%)
    pallas_call x1, Pallas kernels, shards(): pl.pallas_call(kernel, out_shape=jax.ShapeDtypeStruct((64, CM), f32), in_...  91.6 us

profile of v7, /device:TPU:1, one launch (start us, length us, event | category | flops | bytes accessed | tf_op | source)
XLA Modules:
  0.0 93.1 jit_solution(10125932028541995532)
XLA Ops:
  0.0 91.6 %shard_map.55 = f32[64,256]{1,0:T(8,128)} custom-call(f32[8]{0:T(128)} %var_hbm.1, bf16[3072,256]{1,0:T(8,128)(2,1)} %m_hbm.1, f32[1,3072]{1,0:T(1,128)} %bitcast.2, s32[1,3072]{1,0:T(1,128)} %bitcast.3, f32[64,256]{1,0:T(8,128)} %ens_hbm.1), custom_call_target="tpu_custom_call" | custom-call | tf_op jit(solution)/shard_map/pallas_call | solution.py:609
  91.6 1.5 %copy.7 = f32[64,256]{1,0:T(8,128)} copy(f32[64,256]{1,0:T(8,128)} %shard_map.55) | data formatting | bytes 131072

commit v8 on v7

--- a/solution.py
+++ b/solution.py
@@ -31,8 +31,8 @@
 ROWS = tuple(len(blocks) * count for blocks, _, count, _ in PARTS)
 ORDER = (
     (0, 0), (1, 0), "small", (2, 0), "small y", "prev 0", (0, 1), (1, 1), "prev 1", (3, 0), (0, 2),
-    "white prev", (4, 0), (2, 1), (3, 1), (5, 0), (1, 2), "small z", (6, 0), (4, 1), (2, 2), (0, 3),
-    (5, 1), (7, 0), (3, 2), (6, 1), (8, 0), (4, 2), (9, 0), (5, 2), (7, 1), (1, 3), (8, 1), (3, 3), (0, 4),
+    "white prev", (4, 0), (2, 1), (5, 0), (1, 2), "small z", (3, 1), (6, 0), (4, 1), (0, 3), (2, 2),
+    (5, 1), (7, 0), (3, 2), (8, 0), (6, 1), (1, 3), (4, 2), (9, 0), (5, 2), (7, 1), (8, 1), (3, 3), (0, 4),
     (6, 2), (9, 1), (5, 3), (4, 3), (7, 2), (8, 2), (2, 3), (6, 3), (9, 2), (7, 3), "vectors", (5, 4),
     (3, 4), (6, 4), (1, 4), (4, 4), (8, 3), (2, 4), (9, 3), (7, 4),
 )
@@ -41,6 +41,8 @@
 VR = 4
 WIDE = 5 * CM
 N_SEMS = 4 * len(ROWS) + len(CHUNKS) + 1 + PREV + 1 + 3 + 3 + 7 + 2
+OWN = 13
+POOL = 16
 N_LOADS = NS // KT + 4
 FAR_Z = (4, 3, 5, 2, 6, 1, 7)
 NT = (((1,), (1,)), ((), ()))
@@ -81,9 +83,9 @@
     (
         m_ref, obs_ref, cls_ref, var_ref, raw, near, prev, sib, white, white_prev, sums, scale, bases,
         ensemble_in, centers, small, small_y, small_z, small_m, strip, terms, vec, polys, exchange,
-        rows_out, plane, norms, tally, loads, sems,
-    ) = scratch[:30]
-    lists = scratch[30:]
+        rows_out, plane, norms, tally, loads, sends, sems,
+    ) = scratch[:31]
+    lists = scratch[31:]
     n = len(ROWS)
     part, from_y, sum_y, from_z, gather_z = (lists[i * n : (i + 1) * n] for i in range(5))
 
@@ -111,31 +113,40 @@
 
     sibling = (dp, mem + 1 - 2 * k)
     started = []
+    leaving = {}
+
+    def slot(i):
+        return i if i < OWN else OWN + (i - OWN) % POOL
+
+    def left(at):
+        landing = started[leaving.pop(at)]
+        pltpu.make_async_copy(landing, landing, sends.at[at]).wait()
+
 
     def start(group, landing, i=None):
         if i is None:
             i = len(started)
             started.append(landing)
+            if slot(i) in leaving:
+                left(slot(i))
+            leaving[slot(i)] = i
         for src, dst, device in group:
             pltpu.make_async_remote_copy(
                 src_ref=src,
                 dst_ref=dst,
-                send_sem=sems.at[0, i],
-                recv_sem=sems.at[1, i],
+                send_sem=sends.at[slot(i)],
+                recv_sem=sems.at[i],
                 device_id=device,
                 device_id_type=MESH,
             ).start()
         return i
 
     def arrive(i):
-        pltpu.make_async_copy(started[i], started[i], sems.at[1, i]).wait()
-
-    drained = [0]
-
-    def drain():
-        for i in range(drained[0], len(started)):
-            pltpu.make_async_copy(started[i], started[i], sems.at[0, i]).wait()
-        drained[0] = len(started)
+        pltpu.make_async_copy(started[i], started[i], sems.at[i]).wait()
+
+    def drain(before):
+        for at in [at for at, i in leaving.items() if i < before]:
+            left(at)
 
     barrier = pltpu.get_barrier_semaphore()
     greeted = (
@@ -528,9 +539,7 @@
         polys[2 * chip + core] = vec[2 * chip + core]
     before = len(started)
     needed, _ = times(1)
-    for i in range(before):
-        pltpu.make_async_copy(started[i], started[i], sems.at[0, i]).wait()
-    drained[0] = before
+    drain(before)
     arrive(late)
     advanced(0, distant, one_step)
     for chip, core in distant:
@@ -563,7 +572,7 @@
     stored.start()
     arrive(planes)
     stored.wait()
-    drain()
+    drain(len(started))
 
 
 def shards(modelled_reactions, observations, noise_class, class_variance, ensemble):
@@ -599,7 +608,8 @@
         pltpu.VMEM((8, 128), f32),
         pltpu.VMEM((22, VR, CM), f32),
         pltpu.SemaphoreType.DMA((N_LOADS,)),
-        pltpu.SemaphoreType.DMA((2, N_SEMS)),
+        pltpu.SemaphoreType.DMA((OWN + POOL,)),
+        pltpu.SemaphoreType.DMA((N_SEMS,)),
     ]
     scratch += [pltpu.VMEM((r, 512), f32) for r in ROWS]
     scratch += [pltpu.VMEM((NY - 1, r // 4, 512), f32) for r in ROWS]

time: 93.2 us -> 93.5 us (level)
  no operation moved by 1% of the time
where the time goes in v8:
time: 93.5 us; the launch traced here: 93.4 us
  Pallas kernels  91.9 us (98%)
  local copies, waits for them, and re-layouts  1.47 us (2%)
    pallas_call x1, Pallas kernels, shards(): pl.pallas_call(kernel, out_shape=jax.ShapeDtypeStruct((64, CM), f32), in_...  91.9 us

profile of v8, /device:TPU:1, one launch (start us, length us, event | category | flops | bytes accessed | tf_op | source)
XLA Modules:
  0.0 93.4 jit_solution(10572650860184518975)
XLA Ops:
  0.0 91.9 %shard_map.55 = f32[64,256]{1,0:T(8,128)} custom-call(f32[8]{0:T(128)} %var_hbm.1, bf16[3072,256]{1,0:T(8,128)(2,1)} %m_hbm.1, f32[1,3072]{1,0:T(1,128)} %bitcast.2, s32[1,3072]{1,0:T(1,128)} %bitcast.3, f32[64,256]{1,0:T(8,128)} %ens_hbm.1), custom_call_target="tpu_custom_call" | custom-call | tf_op jit(solution)/shard_map/pallas_call | solution.py:619
  91.9 1.5 %copy.7 = f32[64,256]{1,0:T(8,128)} copy(f32[64,256]{1,0:T(8,128)} %shard_map.55) | data formatting | bytes 131072
